TPU v7x, 256 devices: a whole 4x4x8 slice. The times are simulated.
256 devices in a mesh: light: 64 (over z, y, x_hi), depth: 2 (over core), tile: 2 (over x_lo).
Axes of the slice: x: 4 (x_hi: 2, x_lo: 2; x = x_hi * 2 + x_lo), y: 4, z: 8, core: 2. Of those that a mesh axis runs over, the one named last changes fastest.
Arguments:
- density: float32 [2048, 128, 1024], P('light', 'depth', 'tile'), may hold values from 0.05 to 2
- extinction: float32 [3], replicated, may hold values from 1 to 4
- sun_colour: float32 [3], replicated, may hold values from 1 to 3
- sky_colour: float32 [3], replicated, may hold values from 0.2 to 2
Outputs:
- image: float32 [3, 2048, 1024], P(None, ('light', 'depth'), 'tile')
- transmittance: float32 [3, 2048, 1024], P(None, ('light', 'depth'), 'tile')
All inputs are finite; a program needn't handle non-finite values.
Results may differ from a plain program's by a relative error of at most 0.0003.
Values sent between devices are 32-bit elements; how exact they have to be, the bound alone decides.
No kernel may reach another device: no remote copies, remote signals or barrier semaphores. Data moves between devices by JAX's collectives and lax.ppermute only.
A program may use at most 64 MiB of HBM per device.

v0:
```python
import jax
import jax.numpy as jnp
from jax import lax
from jax.sharding import PartitionSpec as P


def prefix(value, axis, combine, identity):
    size, position = (lax.axis_size(axis), lax.axis_index(axis))
    everything = lax.all_gather(value, axis)
    start = jnp.broadcast_to(jnp.asarray(identity, value.dtype), value.shape)

    def hop(k, before):
        reached = k < position
        new = combine(before, everything[k])
        return jnp.where(reached, new, before)

    return lax.fori_loop(0, size, hop, start)


def add_terms(earlier, later):
    return earlier + later


def multiply_terms(earlier, later):
    return earlier * later


def per_device(density, extinction, sun_colour, sky_colour):
    light_count = lax.axis_size("light")
    depth_count = lax.axis_size("depth")
    full_x = density.shape[0] * light_count
    full_y = density.shape[1] * depth_count
    column_view = jnp.sum(density, axis=1)
    passing = jnp.exp(-extinction[:, None, None] * column_view[None] / full_y)
    front_all = prefix(passing, "depth", multiply_terms, jnp.ones_like(passing))
    front_pass = [front_all[colour] for colour in range(3)]
    column_light = jnp.sum(density, axis=0)
    before_light = prefix(column_light, "light", add_terms, jnp.zeros_like(column_light))
    sun_depth = (before_light[None] + jnp.cumsum(density, axis=0) - 0.5 * density) / full_x
    local_view = (jnp.cumsum(density, axis=1) - density) / full_y
    shares = []
    for colour in range(3):
        radiance = sun_colour[colour] * jnp.exp(-extinction[colour] * sun_depth)
        opacity = -jnp.expm1(-extinction[colour] * density / full_y)
        weight = front_pass[colour][:, None, :] * jnp.exp(-extinction[colour] * local_view)
        shares.append(jnp.sum(weight * opacity * radiance, axis=1))
    contribution = jnp.stack(shares)
    summed, column_sum = (
        lax.psum_scatter(contribution, "depth", scatter_dimension=1, tiled=True),
        lax.psum_scatter(column_view[None], "depth", scatter_dimension=1, tiled=True),
    )
    transmittance = jnp.exp(-extinction[:, None, None] * column_sum / full_y)
    image = summed + sky_colour[:, None, None] * transmittance
    return (image, transmittance)


def solution(mesh):
    return jax.shard_map(
        per_device,
        mesh=mesh,
        in_specs=(P("light", "depth", "tile"), P(), P(), P()),
        out_specs=(P(None, ("light", "depth"), "tile"), P(None, ("light", "depth"), "tile")),
        check_vma=False,
    )
```

profile of v0, /device:TPU:1, one launch (start us, length us, event | category | flops | bytes accessed | tf_op | source)
XLA Modules:
  0.0 267.3 jit_solution(18177716318687959617)
XLA Ops:
  8.1 3.6 %fusion.3 = (f32[64,512]{1,0:T(8,128)}, f32[32,512]{1,0:T(8,128)}) fusion(f32[32,64,512]{2,1,0:T(8,128)} %param.8), kind=kLoop, calls=%fused_computation.17 | loop fusion | flops 2048000 | bytes 4390912 | tf_op jit(solution)/shard_map/reduce_sum | solution.py:37
  14.8 4.5 %fusion.6 = f32[32,64,512]{2,1,0:T(8,128)} fusion(f32[32,64,512]{2,1,0:T(8,128)} %param.8), kind=kOutput, calls=%fused_computation.20 | output fusion | flops 32505856 | bytes 8388608 | tf_op jit(solution)/shard_map/jit(cumsum)/reduce_window_sum | solution.py:39
  19.3 5.0 %all_gather.10 = f32[2,3,32,512]{3,2,1,0:T(8,128)S(1)} all-gather(f32[1,3,32,512]{3,2,1,0:T(8,128)S(1)} %multiply_exponential_fusion), channel_id=1, replica_groups=mesh['light'=64,'depth'=2,'tile'=2] {'depth'}, dimensions={0}, use_global_device_ids=true | all-gather | bytes 589824 | tf_op jit(solution)/shard_map/all_gather | solution.py:9
  25.1 139.3 %all-gather.3.cloned.1.call-done = f32[4096,512]{1,0:T(8,128)} async-done(((f32[64,512]{1,0:T(8,128)}), f32[4096,512]{1,0:T(8,128)}) %all-gather.3.cloned.1.call-update) | async-done | bytes 8388624 | tf_op jit(solution)/shard_map/all_gather | solution.py:9
  164.4 62.7 %while.29 = (s32[]{:T(128)}, f32[64,512]{1,0:T(8,128)S(1)}, s32[]{:T(128)}, f32[64,64,512]{2,1,0:T(8,128)}, s32[]{:T(128)}, /*index=5*/s32[]{:T(128)}) while((s32[]{:T(128)}, f32[64,512]{1,0:T(8,128)S(1)}, s32[]{:T(128)}, f32[64,64,512]{2,1,0:T(8,128)}, s32[]{:T(128)}, /*index=5*/s32[]{:T(128)}) %tuple.85), condition=%wide.region_6.7_spmd.clone, body=%wide.region_5.6_spmd.clone.sunk | while | flops 98308 | bytes 393309 | solution.py:17
  165.4 1.0 add_select_fusion.2
  166.4 1.0 add_select_fusion.2
  167.4 1.0 add_select_fusion.2
  168.4 1.0 add_select_fusion.2
  169.3 1.0 add_select_fusion.2
  170.3 1.0 add_select_fusion.2
  171.3 1.0 add_select_fusion.2
  172.3 1.0 add_select_fusion.2
  173.3 1.0 add_select_fusion.2
  174.2 1.0 add_select_fusion.2
  175.2 1.0 add_select_fusion.2
  176.2 1.0 add_select_fusion.2
  177.2 1.0 add_select_fusion.2
  178.2 1.0 add_select_fusion.2
  179.1 1.0 add_select_fusion.2
  180.1 1.0 add_select_fusion.2
  181.1 1.0 add_select_fusion.2
  182.1 1.0 add_select_fusion.2
  183.1 1.0 add_select_fusion.2
  184.0 1.0 add_select_fusion.2
  185.0 1.0 add_select_fusion.2
  186.0 1.0 add_select_fusion.2
  187.0 1.0 add_select_fusion.2
  188.0 1.0 add_select_fusion.2
  188.9 1.0 add_select_fusion.2
  189.9 1.0 add_select_fusion.2
  190.9 1.0 add_select_fusion.2
  191.9 1.0 add_select_fusion.2
  192.9 1.0 add_select_fusion.2
  193.9 1.0 add_select_fusion.2
  194.8 1.0 add_select_fusion.2
  195.8 1.0 add_select_fusion.2
  196.8 1.0 add_select_fusion.2
  197.8 1.0 add_select_fusion.2
  198.8 1.0 add_select_fusion.2
  199.7 1.0 add_select_fusion.2
  201.7 1.0 add_select_fusion.2
  204.6 1.0 add_select_fusion.2
  220.3 1.0 add_select_fusion.2
  223.3 1.0 add_select_fusion.2
  227.2 17.3 %multiply_reduce_fusion.2 = (f32[32,512]{1,0:T(8,128)S(1)}, f32[32,512]{1,0:T(8,128)S(1)}, f32[32,512]{1,0:T(8,128)S(1)}) fusion(f32[32,64,512]{2,1,0:T(8,128)} %param.8, f32[32,64,512]{2,1,0:T(8,128)} %fusion.6, f32[]{:T(128)S(6)} %mul.203, f32[64,512]{1,0:T(8,128)S(1)} %get-tuple-element.161, f32[]{:T(128)} %bitcast.2, f32[]{:T(128)} %bitcast.1, ...), kind=kOutput, calls=%fused_computation.6 | output fusion | flops 101662720 | bytes 8912944 | tf_op jit(solution)/shard_map/jit(cumsum)/reduce_window_sum | solution.py:40
  245.3 12.9 %reduce-scatter.3.cloned.1.call-done = f32[3,16,512]{2,1,0:T(8,128)} async-done(((f32[3,32,512]{2,1,0:T(8,128)}), f32[3,16,512]{2,1,0:T(8,128)}) %reduce-scatter.3.cloned.1.call-update) | async-done | bytes 98320 | tf_op jit(solution)/shard_map/reduce_scatter | solution.py:49
  258.2 1.7 multiply_add_fusion
  (50 shorter events, 26.0 us)
Async XLA Ops:
  8.0 4.3 %copy-start.1 = (f32[3]{0:T(128)S(1)}, f32[3]{0:T(128)}, u32[]{:S(2)}) copy-start(f32[3]{0:T(128)} %param.9) | copy-start | bytes 40
  8.0 156.4 %all-gather.3.cloned.1.call-start = ((), (), s32[]{:S(2)}) async-start(), calls=%async_computation.4 | async-start | bytes 8519680 | tf_op jit(solution)/shard_map/all_gather | solution.py:9
  11.6 233.6 %reduce-scatter.5.cloned.1.call-start = ((), (), s32[]{:S(2)}) async-start(), calls=%async_computation.3 | async-start | bytes 98304 | tf_op jit(solution)/shard_map/reduce_scatter | solution.py:50
  12.2 246.0 %reduce-scatter.3.cloned.1.call-start = ((), (), s32[]{:S(2)}) async-start(), calls=%async_computation.2 | async-start | bytes 294912 | tf_op jit(solution)/shard_map/reduce_scatter | solution.py:49
  14.7 4.5 %copy-start = (f32[32,512]{1,0:T(8,128)S(1)}, f32[32,512]{1,0:T(8,128)}, u32[]{:S(2)}) copy-start(f32[32,512]{1,0:T(8,128)} %get-tuple-element.196) | copy-start | bytes 196612
  19.2 5.3 %copy-start.2 = (f32[3]{0:T(128)S(1)}, f32[3]{0:T(128)}, u32[]{:S(2)}) copy-start(f32[3]{0:T(128)} %param.10) | copy-start | bytes 40
  227.2 31.0 %copy-start.3 = (f32[3]{0:T(128)S(1)}, f32[3]{0:T(128)}, u32[]{:S(2)}) copy-start(f32[3]{0:T(128)} %param.11) | copy-start | bytes 40
Sparse Core Ops, SparseCore 0:
  12.3 152.0 all-gather.2
Sparse Core Ops, SparseCore 1:
  15.1 17.2 reduce-scatter.4
  245.3 12.8 reduce-scatter.2
where the time goes:
time: 269 us; the launch traced here: 267 us
  waiting for transfers between devices  153 us (57%)
  other arithmetic  89.2 us (33%)
  between operations  17.4 us (6%)
  blocking collectives  4.96 us (2%)
    all_gather x1, waiting for transfers between devices, prefix(): everything = lax.all_gather(value, axis)  139 us
    select_n x66, other arithmetic, hop(): return jnp.where(reached, new, before)  61.4 us
    another operation x1, other arithmetic, per_device(): local_view = (jnp.cumsum(density, axis=1) - density) / full_y  17.3 us
    reduce_scatter x1, waiting for transfers between devices, per_device(): lax.psum_scatter(contribution, 'depth', scatter_dimension=1, tiled=True)  12.9 us
  transfers between devices with their start and end apart: 3, of which 2 were waited for; matrix products, arithmetic and copies ran while one was open for 32% of the time, Pallas kernels for 0%

commit v1 on v0

v1 whole, which is shorter than its diff:
```python
import functools

import jax
import jax.numpy as jnp
from jax import lax
from jax.experimental import pallas as pl
from jax.experimental.pallas import tpu as pltpu
from jax.sharding import Mesh
from jax.sharding import PartitionSpec as P

PLANE = ("y", "x")
LANES = 128
VMEM = pl.BlockSpec(memory_space=pltpu.VMEM)
SMEM = pl.BlockSpec(memory_space=pltpu.SMEM)


def params(mib):
    return pltpu.CompilerParams(vmem_limit_bytes=mib * 1024 * 1024)


def column_kernel(density_ref, sum_ref):
    @pl.when(pl.program_id(0) == 0)
    def _():
        sum_ref[...] = jnp.zeros_like(sum_ref)

    sum_ref[...] += jnp.sum(density_ref[...], axis=0)


def column_light_of(density):
    nx, ny, nz = density.shape
    chunk = 8
    return pl.pallas_call(
        column_kernel,
        grid=(nx // chunk,),
        in_specs=[pl.BlockSpec((chunk, ny, nz), lambda i: (i, 0, 0))],
        out_specs=pl.BlockSpec((ny, nz), lambda i: (0, 0)),
        out_shape=jax.ShapeDtypeStruct((ny, nz), jnp.float32),
        compiler_params=params(16),
        name="column_light",
    )(density)


def view_kernel(density_ref, sum_ref):
    sum_ref[...] = jnp.sum(density_ref[...], axis=1)


def column_view_of(density):
    nx, ny, nz = density.shape
    chunk = 8
    return pl.pallas_call(
        view_kernel,
        grid=(nx // chunk,),
        in_specs=[pl.BlockSpec((chunk, ny, nz), lambda i: (i, 0, 0))],
        out_specs=pl.BlockSpec((chunk, nz), lambda i: (i, 0)),
        out_shape=jax.ShapeDtypeStruct((nx, nz), jnp.float32),
        compiler_params=params(16),
        cost_estimate=pl.CostEstimate(flops=2**20, bytes_accessed=2**22, transcendentals=0),
        name="column_view",
    )(density)


def brick_kernel(sizes, ext_ref, front_ref, d_ref, g_ref, s_ref):
    nx, ny, full_x, full_y = sizes
    lanes = pl.ds(pl.multiple_of(pl.program_id(0) * LANES, LANES), LANES)

    def along_x(i, _):
        carry = jnp.zeros((8, LANES), jnp.float32)
        for x in range(nx):
            at = pl.ds(pl.multiple_of(x * ny + i * 8, 8), 8)
            cell = d_ref[at, :]
            s_ref[at, :] = carry + 0.5 * cell
            carry = carry + cell
        return 0

    lax.fori_loop(0, ny // 8, along_x, 0)

    def along_y(i, _):
        xs = pl.multiple_of(i * 8, 8)
        view = front_ref[pl.ds(xs, 8), :]
        passing = [jnp.exp(view * (-ext_ref[c] / full_y)) for c in range(3)]

        def cells(step, state):
            view, passing = state
            passing = list(passing)
            for k in range(8):
                y = step * 8 + k
                at = pl.ds(xs * ny + y, 8, stride=ny)
                view = view + d_ref[at, :]
                sun = s_ref[at, :]
                for c in range(3):
                    later = jnp.exp(view * (-ext_ref[c] / full_y))
                    g_ref[c, y, pl.ds(xs, 8), lanes] = (passing[c] - later) * jnp.exp(sun * (-ext_ref[c] / full_x))
                    passing[c] = later
            return view, tuple(passing)

        lax.fori_loop(0, ny // 8, cells, (view, tuple(passing)))
        return 0

    lax.fori_loop(0, nx // 8, along_y, 0)


def brick_light_of(density, front, extinction, full_x, full_y):
    nx, ny, nz = density.shape
    return pl.pallas_call(
        functools.partial(brick_kernel, (nx, ny, full_x, full_y)),
        grid=(nz // LANES,),
        in_specs=[
            SMEM,
            pl.BlockSpec((nx, LANES), lambda i: (0, i)),
            pl.BlockSpec((nx * ny, LANES), lambda i: (0, i)),
        ],
        out_specs=VMEM,
        out_shape=pltpu.VMEM((3, ny, nx, nz), jnp.float32),
        scratch_shapes=[pltpu.VMEM((nx * ny, LANES), jnp.float32)],
        compiler_params=params(16),
        cost_estimate=pl.CostEstimate(flops=2**25, bytes_accessed=2**24, transcendentals=6 * 2**20),
        name="brick_light",
    )(extinction, front, density.reshape(nx * ny, nz))


def pixel_kernel(sizes, half_ref, ext_ref, sun_ref, before_ref, g_ref, out_ref, a_ref):
    nx, ny, nz, full_x = sizes
    tiles = nz // LANES
    rows = nx // 2
    for c in range(3):
        a_ref[c] = sun_ref[c] * jnp.exp(before_ref[...] * (-ext_ref[c] / full_x))
    base = pl.multiple_of(half_ref[0] * rows, 8)

    def pixels(i, _):
        lanes = pl.ds(pl.multiple_of((i % tiles) * LANES, LANES), LANES)
        c = i // tiles
        total = [jnp.zeros((8, LANES), jnp.float32) for _ in range(rows // 8)]
        for y in range(ny):
            light = jnp.broadcast_to(a_ref[c, pl.ds(y, 1), lanes], (8, LANES))
            for t in range(rows // 8):
                total[t] = total[t] + light * g_ref[c, y, pl.ds(base + 8 * t, 8), lanes]
        for t in range(rows // 8):
            out_ref[c, 8 * t : 8 * t + 8, lanes] = total[t]
        return 0

    lax.fori_loop(0, 3 * tiles, pixels, 0)


def pixels_of(half, brick, before, extinction, sun_colour, full_x, name):
    _, ny, nx, nz = brick.shape
    return pl.pallas_call(
        functools.partial(pixel_kernel, (nx, ny, nz, full_x)),
        in_specs=[SMEM, SMEM, SMEM, VMEM, VMEM],
        out_specs=VMEM,
        out_shape=jax.ShapeDtypeStruct((3, nx // 2, nz), jnp.float32),
        scratch_shapes=[pltpu.VMEM((3, ny, nz), jnp.float32)],
        compiler_params=params(4),
        cost_estimate=pl.CostEstimate(flops=2**21, bytes_accessed=2**22, transcendentals=2**16),
        name=name,
    )(half, extinction, sun_colour, before, pltpu.with_memory_space_constraint(brick, pltpu.VMEM))


def light_before(column_light, sizes):
    planes, members = sizes
    ny, nz = column_light.shape
    part = ny // members
    own = lax.all_to_all(column_light.reshape(members, part, nz), PLANE, 0, 0, tiled=True)
    within = [jnp.zeros_like(own[0])]
    for k in range(members):
        within.append(within[-1] + own[k])
    plane_sum = within.pop()
    sums = lax.all_to_all(jnp.broadcast_to(plane_sum[None], (planes, part, nz)), "z", 0, 0, tiled=True)
    plane = lax.axis_index("z")
    nearer = jnp.zeros_like(plane_sum)
    for k in range(planes):
        nearer = nearer + jnp.where(k < plane, sums[k], 0.0)
    back = jnp.stack([value + nearer for value in within])
    return lax.all_to_all(back, PLANE, 0, 0, tiled=True).reshape(ny, nz)


def per_device(sizes, density, extinction, sun_colour, sky_colour):
    planes, members, full_x, full_y = sizes
    nx = density.shape[0]
    half = lax.axis_index("depth").astype(jnp.int32)
    swap = functools.partial(lax.ppermute, axis_name="depth", perm=[(0, 1), (1, 0)])
    column_light = column_light_of(density)
    before = light_before(column_light, (planes, members))
    column_view = column_view_of(density)
    other_view = swap(column_view)
    front = jnp.where(half == 1, other_view, 0.0)
    own_rows = lax.dynamic_slice_in_dim(column_view + other_view, half * (nx // 2), nx // 2, 0)
    transmittance = jnp.exp(-extinction[:, None, None] * own_rows[None] / full_y)
    background = sky_colour[:, None, None] * transmittance
    brick = brick_light_of(density, front, extinction, full_x, full_y)
    sent = pixels_of((1 - half).reshape(1), brick, before, extinction, sun_colour, full_x, "pixels_sent")
    received = swap(sent)
    kept = pixels_of(half.reshape(1), brick, before, extinction, sun_colour, full_x, "pixels_kept")
    return kept + received + background, transmittance


def solution(mesh):
    shape = (8, 4, 2, 2, 2)
    fine = Mesh(mesh.devices.reshape(shape), ("z", "y", "x", "depth", "tile"))
    light = ("z", "y", "x")
    sizes = (8, 8, 2048, 128)
    return jax.shard_map(
        functools.partial(per_device, sizes),
        mesh=fine,
        in_specs=(P(light, "depth", "tile"), P(), P(), P()),
        out_specs=(P(None, (*light, "depth"), "tile"), P(None, (*light, "depth"), "tile")),
        check_vma=False,
    )
```

time: 269 us -> 75.6 us (0.28)
  the two profiles are of different devices: /device:TPU:1 before, /device:TPU:4 now
where the time goes in v1:
time: 75.6 us; the launch traced here: 75.1 us
  local copies, waits for them, and re-layouts  19.2 us (25%)
  Pallas kernels  15.8 us (21%)
  starting transfers between devices  14.7 us (19%)
  blocking collectives  12.6 us (17%)
  other arithmetic  6.31 us (8%)
  waiting for transfers between devices  5.65 us (7%)
  between operations  0.77 us (1%)
    unnamed x20, local copies, waits for them, and re-layouts  18.6 us
    all_to_all x1, blocking collectives, light_before(): lax.all_to_all(column_light.reshape(members, part, nz), PLANE, 0, 0, tile...  12.6 us
    pallas_call x1, Pallas kernels, brick_light_of(): pl.pallas_call(functools.partial(brick_kernel, (nx, ny, full_x, full_y)),...  10.7 us
    all_to_all x1, starting transfers between devices, light_before(): lax.all_to_all(jnp.broadcast_to(plane_sum[None], (planes, part, nz)), 'z'...  8.47 us
    all_to_all x1, starting transfers between devices, light_before(): return lax.all_to_all(back, PLANE, 0, 0, tiled=True).reshape(ny, nz)  6.06 us
    all_to_all x1, waiting for transfers between devices, light_before(): lax.all_to_all(jnp.broadcast_to(plane_sum[None], (planes, part, nz)), 'z'...  5.64 us
    pallas_call x2, Pallas kernels, pixels_of(): pl.pallas_call(functools.partial(pixel_kernel, (nx, ny, nz, full_x)), in_...  4.4 us
    unnamed x7, other arithmetic  4.24 us
  transfers between devices with their start and end apart: 4, of which 1 were waited for; matrix products, arithmetic and copies ran while one was open for 7% of the time, Pallas kernels for 18%

profile of v1, /device:TPU:4, one launch (start us, length us, event | category | flops | bytes accessed | tf_op | source)
XLA Modules:
  0.0 75.1 jit_solution(18137359499124487001)
XLA Ops:
  0.6 0.0 copy-start.3
  0.6 2.2 %copy-done.3 = f32[32,64,512]{2,1,0:T(8,128)S(1)} copy-done((f32[32,64,512]{2,1,0:T(8,128)S(1)}, f32[32,64,512]{2,1,0:T(8,128)}, u32[]{:S(2)}) %copy-start.3) | copy-done | bytes 4194328
  2.8 0.0 copy-start.7
  2.8 0.0 copy-start.8
  2.8 0.3 column_light.1
  3.1 12.6 %all_to_all.15 = f32[8,8,512]{2,1,0:T(8,128)S(1)} all-to-all(f32[8,8,512]{2,1,0:T(8,128)S(1)} %bitcast.10), channel_id=1, replica_groups=mesh['z'=8,'y'=4,'x'=2,'depth'=2,'tile'=2] {'y','x'}, dimensions={0} | all-to-all | bytes 262144 | tf_op jit(solution)/shard_map/all_to_all | solution.py:162
  15.8 0.7 broadcast_in_dim.27
  16.4 8.5 %all-to-all-start.1 = ((f32[8,8,512]{2,1,0:T(8,128)}), f32[8,8,512]{2,1,0:T(8,128)S(1)}, u32[]{:S(2)}, u32[]{:S(2)}) async-start(f32[8,8,512]{2,1,0:T(8,128)} %broadcast_in_dim.27), calls=%async_computation.1 | async-start | bytes 262144 | tf_op jit(solution)/shard_map/all_to_all | solution.py:167
  24.9 0.0 copy-start.4
  24.9 2.2 %copy-done.4 = f32[32,64,512]{2,1,0:T(8,128)S(1)} copy-done((f32[32,64,512]{2,1,0:T(8,128)S(1)}, f32[32,64,512]{2,1,0:T(8,128)}, u32[]{:S(2)}) %copy-start.4) | copy-done | bytes 4194328
  27.1 0.5 column_view.1
  27.6 0.1 collective-permute-start
  27.7 0.7 neg.4
  28.3 5.6 %all-to-all-done.1 = f32[8,8,512]{2,1,0:T(8,128)S(1)} async-done(((f32[8,8,512]{2,1,0:T(8,128)}), f32[8,8,512]{2,1,0:T(8,128)S(1)}, u32[]{:S(2)}, u32[]{:S(2)}) %all-to-all-start.1) | async-done | bytes 131104 | tf_op jit(solution)/shard_map/all_to_all | solution.py:167
  34.0 0.6 constant_dynamic-update-slice_fusion.7
  34.6 0.6 constant_dynamic-update-slice_fusion.6
  35.2 0.6 constant_dynamic-update-slice_fusion.5
  35.8 0.6 constant_dynamic-update-slice_fusion.4
  36.4 0.6 constant_dynamic-update-slice_fusion.3
  37.0 0.6 constant_dynamic-update-slice_fusion.2
  37.6 0.6 constant_dynamic-update-slice_fusion.1
  38.2 0.6 constant_dynamic-update-slice_fusion
  38.8 6.1 %all-to-all-start.2 = ((f32[8,8,512]{2,1,0:T(8,128)}), f32[8,8,512]{2,1,0:T(8,128)S(1)}, u32[]{:S(2)}, u32[]{:S(2)}) async-start(f32[8,8,512]{2,1,0:T(8,128)} %constant_dynamic-update-slice_fusion), calls=%async_computation.2 | async-start | bytes 262144 | tf_op jit(solution)/shard_map/all_to_all | solution.py:173
  44.9 0.0 collective-permute-done
  44.9 0.0 copy-start.5
  44.9 2.2 %copy-done.5 = f32[32,64,512]{2,1,0:T(8,128)S(1)} copy-done((f32[32,64,512]{2,1,0:T(8,128)S(1)}, f32[32,64,512]{2,1,0:T(8,128)}, u32[]{:S(2)}) %copy-start.5) | copy-done | bytes 4194328
  47.1 0.0 copy-start.6
  47.1 0.7 copy-done.6
  47.8 10.7 %brick_light.1.g_ref = f32[3,64,32,512]{3,2,1,0:T(8,128)S(1)} custom-call(f32[3]{0:T(128)S(1)} %copy-done.6, f32[32,512]{1,0:T(8,128)S(1)} %broadcast_select_fusion.front_ref, f32[2048,512]{1,0:T(8,128)S(1)} %bitcast.7), custom_call_target="tpu_custom_call" | custom-call | flops 33554432 | bytes 16777216 | tf_op jit(solution)/shard_map/brick_light/pallas_call | solution.py:104
  58.5 0.0 copy-start
  58.5 4.5 %copy-done = f32[3,64,32,512]{3,2,1,0:T(8,128)} copy-done((f32[3,64,32,512]{3,2,1,0:T(8,128)}, f32[3,64,32,512]{3,2,1,0:T(8,128)S(1)}, u32[]{:S(2)}) %copy-start) | copy-done | bytes 12582936
  63.0 0.0 all-to-all-done.2
  63.0 0.0 copy-done.7
  63.0 0.0 copy-done.8
  63.0 0.0 copy-start.1
  63.0 4.6 %copy-done.1 = f32[3,64,32,512]{3,2,1,0:T(8,128)S(1)} copy-done((f32[3,64,32,512]{3,2,1,0:T(8,128)S(1)}, f32[3,64,32,512]{3,2,1,0:T(8,128)}, u32[]{:S(2)}) %copy-start.1) | copy-done | bytes 12582936
  67.6 0.0 copy-start.2
  67.6 0.0 copy-start.9
  67.6 2.2 %pixels_sent.1 = f32[3,16,512]{2,1,0:T(8,128)S(1)} custom-call(s32[1]{0:T(128)} %bitcast.5.half_ref, f32[3]{0:T(128)S(1)} %copy-done.7, f32[3]{0:T(128)S(1)} %copy-done.8, f32[64,512]{1,0:T(8,128)S(1)} %bitcast.8, f32[3,64,32,512]{3,2,1,0:T(8,128)S(1)} %copy-done.1), custom_call_target="tpu_custom_call" | custom-call | flops 2097152 | bytes 4194304 | tf_op jit(solution)/shard_map/pixels_sent/pallas_call | solution.py:146
  69.8 0.1 collective-permute-start.1
  69.9 2.3 %copy-done.2 = f32[3,64,32,512]{3,2,1,0:T(8,128)S(1)} copy-done((f32[3,64,32,512]{3,2,1,0:T(8,128)S(1)}, f32[3,64,32,512]{3,2,1,0:T(8,128)}, u32[]{:S(2)}) %copy-start.2) | copy-done | bytes 12582936
  72.1 2.2 %pixels_kept.1 = f32[3,16,512]{2,1,0:T(8,128)S(1)} custom-call(s32[1]{0:T(128)} %bitcast.half_ref, f32[3]{0:T(128)S(1)} %copy-done.7, f32[3]{0:T(128)S(1)} %copy-done.8, f32[64,512]{1,0:T(8,128)S(1)} %bitcast.9, f32[3,64,32,512]{3,2,1,0:T(8,128)S(1)} %copy-done.2), custom_call_target="tpu_custom_call" | custom-call | flops 2097152 | bytes 4194304 | tf_op jit(solution)/shard_map/pixels_kept/pallas_call | solution.py:146
  74.3 0.0 collective-permute-done.1
  74.3 0.0 copy-done.9
  74.3 0.8 %multiply_add_fusion = (f32[3,16,512]{2,1,0:T(8,128)}, f32[3,16,512]{2,1,0:T(8,128)}) fusion(f32[3,16,512]{2,1,0:T(8,128)S(1)} %pixels_kept.1, f32[3,16,512]{2,1,0:T(8,128)S(1)} %collective-permute-done.1, f32[3]{0:T(128)S(1)} %copy-done.9, f32[16,512]{1,0:T(8,128)S(1)} %dynamic-slice_add_fusion, f32[3]{0:T(128)S(1)} %neg.4), kind=kLoop, calls=%fused_computation | loop fusion | flops 122880 | bytes 426008 | tf_op jit(solution)/shard_map/add | solution.py:193
  (3 shorter events, 0.0 us)
Async XLA Ops:
  0.6 2.2 %copy-start.3 = (f32[32,64,512]{2,1,0:T(8,128)S(1)}, f32[32,64,512]{2,1,0:T(8,128)}, u32[]{:S(2)}) copy-start(f32[32,64,512]{2,1,0:T(8,128)} %density_ref.3) | copy-start | bytes 12582916
  2.8 60.2 %copy-start.7 = (f32[3]{0:T(128)S(1)}, f32[3]{0:T(128)}, u32[]{:S(2)}) copy-start(f32[3]{0:T(128)} %ext_ref.5) | copy-start | bytes 40
  2.8 60.2 %copy-start.8 = (f32[3]{0:T(128)S(1)}, f32[3]{0:T(128)}, u32[]{:S(2)}) copy-start(f32[3]{0:T(128)} %sun_ref.3) | copy-start | bytes 40
  16.4 17.5 %all-to-all-start.1 = ((f32[8,8,512]{2,1,0:T(8,128)}), f32[8,8,512]{2,1,0:T(8,128)S(1)}, u32[]{:S(2)}, u32[]{:S(2)}) async-start(f32[8,8,512]{2,1,0:T(8,128)} %broadcast_in_dim.27), calls=%async_computation.1 | async-start | bytes 262144 | tf_op jit(solution)/shard_map/all_to_all | solution.py:167
  24.9 2.2 %copy-start.4 = (f32[32,64,512]{2,1,0:T(8,128)S(1)}, f32[32,64,512]{2,1,0:T(8,128)}, u32[]{:S(2)}) copy-start(f32[32,64,512]{2,1,0:T(8,128)} %density_ref.3) | copy-start | bytes 12582916
  27.6 17.3 %collective-permute-start = (f32[32,512]{1,0:T(8,128)S(1)}, f32[32,512]{1,0:T(8,128)S(1)}, u32[]{:S(2)}, u32[]{:S(2)}) collective-permute-start(f32[32,512]{1,0:T(8,128)S(1)} %column_view.1), channel_id=1, source_target_pairs={{0,2},{2,0},{1,3},{3,1},{4,6},{6,4},{5,7},{7,5},{8,10},{10,8},{9,1... | collective-permute-start | bytes 196616 | tf_op jit(solution)/shard_map/ppermute | solution.py:184
  38.8 24.1 %all-to-all-start.2 = ((f32[8,8,512]{2,1,0:T(8,128)}), f32[8,8,512]{2,1,0:T(8,128)S(1)}, u32[]{:S(2)}, u32[]{:S(2)}) async-start(f32[8,8,512]{2,1,0:T(8,128)} %constant_dynamic-update-slice_fusion), calls=%async_computation.2 | async-start | bytes 262144 | tf_op jit(solution)/shard_map/all_to_all | solution.py:173
  44.9 2.2 %copy-start.5 = (f32[32,64,512]{2,1,0:T(8,128)S(1)}, f32[32,64,512]{2,1,0:T(8,128)}, u32[]{:S(2)}) copy-start(f32[32,64,512]{2,1,0:T(8,128)} %density_ref.3) | copy-start | bytes 12582916
  47.1 0.7 copy-start.6
  58.5 4.5 %copy-start = (f32[3,64,32,512]{3,2,1,0:T(8,128)}, f32[3,64,32,512]{3,2,1,0:T(8,128)S(1)}, u32[]{:S(2)}) copy-start(f32[3,64,32,512]{3,2,1,0:T(8,128)S(1)} %brick_light.1.g_ref) | copy-start | bytes 37748740
  63.0 4.6 %copy-start.1 = (f32[3,64,32,512]{3,2,1,0:T(8,128)S(1)}, f32[3,64,32,512]{3,2,1,0:T(8,128)}, u32[]{:S(2)}) copy-start(f32[3,64,32,512]{3,2,1,0:T(8,128)} %copy-done) | copy-start | bytes 37748740
  67.6 4.6 %copy-start.2 = (f32[3,64,32,512]{3,2,1,0:T(8,128)S(1)}, f32[3,64,32,512]{3,2,1,0:T(8,128)}, u32[]{:S(2)}) copy-start(f32[3,64,32,512]{3,2,1,0:T(8,128)} %copy-done) | copy-start | bytes 37748740
  67.6 6.8 %copy-start.9 = (f32[3]{0:T(128)S(1)}, f32[3]{0:T(128)}, u32[]{:S(2)}) copy-start(f32[3]{0:T(128)} %param.7) | copy-start | bytes 40
  69.8 4.6 %collective-permute-start.1 = (f32[3,16,512]{2,1,0:T(8,128)S(1)}, f32[3,16,512]{2,1,0:T(8,128)S(1)}, u32[]{:S(2)}, u32[]{:S(2)}) collective-permute-start(f32[3,16,512]{2,1,0:T(8,128)S(1)} %pixels_sent.1), channel_id=1, source_target_pairs={{0,2},{2,0},{1,3},{3,1},{4,6},{6,4},{5,7},{7,5},{8,10},{10,8},{9,1... | collective-permute-start | bytes 294920 | tf_op jit(solution)/shard_map/ppermute | solution.py:191

commit v2 on v0

v2 whole, which is shorter than its diff:
```python
import functools

import jax
import jax.numpy as jnp
from jax import lax
from jax.experimental import pallas as pl
from jax.experimental.pallas import tpu as pltpu
from jax.sharding import PartitionSpec as P

LANES = 128
CHUNKS = 8
LOG2E = 1.4426950408889634
VMEM = pl.BlockSpec(memory_space=pltpu.VMEM)
HBM = pl.BlockSpec(memory_space=pltpu.HBM)


def params(mib):
    return pltpu.CompilerParams(vmem_limit_bytes=mib * 1024 * 1024)


def cost(flops, size, transcendentals=0):
    return pl.CostEstimate(flops=flops, bytes_accessed=size, transcendentals=transcendentals)


def load_kernel(sizes, density_ref, ext_ref, sun_ref, sky_ref, light_ref, view_ref, table_ref, held_ref, sums_ref, three_ref, sems, small_sems):
    nx, ny, full_x, full_y = sizes
    tiles = held_ref.shape[0]
    planes = nx // CHUNKS
    rows = planes * ny
    copies = [
        [
            pltpu.make_async_copy(
                density_ref.at[pl.ds(k * rows, rows), pl.ds(t * LANES, LANES)],
                held_ref.at[t, pl.ds(k * rows, rows)],
                sems.at[k, t],
            )
            for t in range(tiles)
        ]
        for k in range(CHUNKS)
    ]
    for chunk in copies:
        for copy in chunk:
            copy.start()
    small = [
        pltpu.make_async_copy(source, three_ref.at[i], small_sems.at[i]) for i, source in enumerate((ext_ref, sun_ref, sky_ref))
    ]
    for copy in small:
        copy.start()
    for k in range(CHUNKS):
        for t in range(tiles):
            copies[k][t].wait()
            block = held_ref[t, k * rows : (k + 1) * rows].reshape(planes, ny, LANES)
            part = jnp.sum(block, axis=0)
            sums_ref[t] = part if k == 0 else sums_ref[t] + part
            view_ref[k * planes : (k + 1) * planes, t * LANES : (t + 1) * LANES] = jnp.sum(block, axis=1)
    for t in range(tiles):
        light_ref[pl.ds(t, ny, stride=tiles), :] = sums_ref[t]
    for copy in small:
        copy.wait()
    for c in range(3):
        row = (-LOG2E / full_y * three_ref[0, c], -LOG2E / full_x * three_ref[0, c], three_ref[1, c], three_ref[2, c])
        for i, value in enumerate(row):
            table_ref[8 * (4 * c + i) : 8 * (4 * c + i) + 8] = jnp.full((8, LANES), value, jnp.float32)


def factor(table_ref, c, which):
    return table_ref[8 * (4 * c + which) : 8 * (4 * c + which) + 8]


def load_of(density, extinction, sun_colour, sky_colour, full_x, full_y):
    nx, ny, nz = density.shape
    tiles = nz // LANES
    return pl.pallas_call(
        functools.partial(load_kernel, (nx, ny, full_x, full_y)),
        in_specs=[HBM, HBM, HBM, HBM],
        out_specs=[VMEM, VMEM, VMEM],
        out_shape=[
            jax.ShapeDtypeStruct((ny * tiles, LANES), jnp.float32),
            jax.ShapeDtypeStruct((nx, nz), jnp.float32),
            jax.ShapeDtypeStruct((12 * 8, LANES), jnp.float32),
        ],
        scratch_shapes=[
            pltpu.VMEM((tiles, nx * ny, LANES), jnp.float32),
            pltpu.VMEM((tiles, ny, LANES), jnp.float32),
            pltpu.SMEM((3, 3), jnp.float32),
            pltpu.SemaphoreType.DMA((CHUNKS, tiles)),
            pltpu.SemaphoreType.DMA((3,)),
        ],
        compiler_params=params(8),
        cost_estimate=cost(2**21, 2**23),
        name="load",
    )(*(pltpu.with_memory_space_constraint(x, pltpu.HBM) for x in (density.reshape(nx * ny, nz), extinction, sun_colour, sky_colour)))


def before_kernel(each, own_ref, *refs):
    before_ref = refs[-1]
    upper = lax.broadcasted_iota(jnp.int32, (8, LANES), 0) >= each
    carry = jnp.zeros((8, LANES), jnp.float32)
    for k in range(own_ref.shape[0] // 8):
        block = own_ref[8 * k : 8 * k + 8]
        other = pltpu.roll(block, each, 0)
        before_ref[8 * k : 8 * k + 8] = carry + jnp.where(upper, other, 0.0)
        carry = carry + (block + other)


def before_of(own, each, after):
    return pl.pallas_call(
        functools.partial(before_kernel, each),
        in_specs=[VMEM] * (1 + len(after)),
        out_specs=VMEM,
        out_shape=jax.ShapeDtypeStruct(own.shape, jnp.float32),
        compiler_params=params(2),
        cost_estimate=cost(2**17, 2**26),
        name="before",
    )(own, *after)


def brick_kernel(nx, ny, table_ref, other_ref, d_ref, g_ref, done_ref, s_ref):
    behind = lax.axis_index("depth").astype(jnp.float32)
    done_ref[...] = jnp.zeros_like(done_ref)
    wide = 32

    def along_x(part, _):
        carry = jnp.zeros((wide, LANES), jnp.float32)
        for x in range(nx):
            at = pl.ds(pl.multiple_of(x * ny + part * wide, 8), wide)
            cell = d_ref[at, :]
            s_ref[at, :] = carry + 0.5 * cell
            carry = carry + cell
        return 0

    lax.fori_loop(0, ny // wide, along_x, 0)

    def along_y(i, _):
        xs = pl.multiple_of(i * 8, 8)
        view_rate = [factor(table_ref, c, 0) for c in range(3)]
        sun_rate = [factor(table_ref, c, 1) for c in range(3)]
        view = other_ref[pl.ds(xs, 8), :] * behind
        passing = [jnp.exp2(view * view_rate[c]) for c in range(3)]

        def cells(step, state):
            view, passing = state
            passing = list(passing)
            for k in range(8):
                y = step * 8 + k
                at = pl.ds(xs * ny + y, 8, stride=ny)
                view = view + d_ref[at, :]
                sun = s_ref[at, :]
                for c in range(3):
                    later = jnp.exp2(view * view_rate[c])
                    g_ref[0, c, y, pl.ds(xs, 8), :] = (passing[c] - later) * jnp.exp2(sun * sun_rate[c])
                    passing[c] = later
            return view, tuple(passing)

        lax.fori_loop(0, ny // 8, cells, (view, tuple(passing)))
        return 0

    lax.fori_loop(0, nx // 8, along_y, 0)


def brick_light_of(density, other_view, table):
    nx, ny, nz = density.shape
    return pl.pallas_call(
        functools.partial(brick_kernel, nx, ny),
        grid=(nz // LANES,),
        in_specs=[
            VMEM,
            pl.BlockSpec((nx, LANES), lambda i: (0, i)),
            pl.BlockSpec((nx * ny, LANES), lambda i: (0, i)),
        ],
        out_specs=[pl.BlockSpec((1, 3, ny, nx, LANES), lambda i: (i, 0, 0, 0, 0)), VMEM],
        out_shape=[
            pltpu.HBM((nz // LANES, 3, ny, nx, LANES), jnp.float32),
            jax.ShapeDtypeStruct((8, LANES), jnp.float32),
        ],
        scratch_shapes=[pltpu.VMEM((nx * ny, LANES), jnp.float32)],
        compiler_params=params(16),
        cost_estimate=cost(2**25, 2**24, 6 * 2**20),
        name="brick_light",
    )(table, other_view, pltpu.with_memory_space_constraint(density.reshape(nx * ny, nz), pltpu.HBM))


def sky_kernel(table_ref, view_ref, other_ref, passed_ref, behind_ref):
    _, rows, nz = passed_ref.shape
    start = lax.axis_index("depth") * rows
    for row in range(0, rows, 8):
        at = pl.ds(pl.multiple_of(start + row, 8), 8)
        for lane in range(0, nz, LANES):
            column = view_ref[at, lane : lane + LANES] + other_ref[at, lane : lane + LANES]
            for c in range(3):
                passed = jnp.exp2(column * factor(table_ref, c, 0))
                passed_ref[c, row : row + 8, lane : lane + LANES] = passed
                behind_ref[c, row : row + 8, lane : lane + LANES] = factor(table_ref, c, 3) * passed


def sky_of(view, other, table):
    nx, nz = view.shape
    shape = jax.ShapeDtypeStruct((3, nx // 2, nz), jnp.float32)
    return pl.pallas_call(
        sky_kernel,
        in_specs=[VMEM, VMEM, VMEM],
        out_specs=[VMEM, VMEM],
        out_shape=[shape, shape],
        compiler_params=params(2),
        name="sky",
    )(table, view, other)


def pixel_kernel(own, table_ref, before_ref, *refs):
    g_ref, start_ref, out_ref, a_ref = refs[0], refs[1:-2], refs[-2], refs[-1]
    tiles, _, ny, nx, _ = g_ref.shape
    rows = nx // 2
    for c in range(3):
        rate, colour = factor(table_ref, c, 1), factor(table_ref, c, 2)
        for row in range(0, before_ref.shape[0], 8):
            a_ref[c, row : row + 8] = colour * jnp.exp2(before_ref[row : row + 8] * rate)
    half = lax.axis_index("depth")
    base = pl.multiple_of((half if own else 1 - half) * rows, 8)
    ways = 4
    for tile in range(tiles):
        at = slice(tile * LANES, (tile + 1) * LANES)

        def pixels(c, _, tile=tile, at=at):
            total = [jnp.zeros((rows, LANES), jnp.float32) for _ in range(ways)]
            for y in range(ny):
                light = jnp.broadcast_to(a_ref[c, pl.ds(y * tiles + tile, 1), :], (rows, LANES))
                total[y % ways] = total[y % ways] + light * g_ref[tile, c, y, pl.ds(base, rows), :]
            value = (total[0] + total[1]) + (total[2] + total[3])
            out_ref[c, :, at] = value + start_ref[0][c, :, at] if start_ref else value
            return 0

        lax.fori_loop(0, 3, pixels, 0)


def pixels_of(own, brick, before, table, name, *start):
    tiles, _, ny, nx, _ = brick.shape
    return pl.pallas_call(
        functools.partial(pixel_kernel, own),
        in_specs=[VMEM] * (3 + len(start)),
        out_specs=VMEM,
        out_shape=jax.ShapeDtypeStruct((3, nx // 2, tiles * LANES), jnp.float32),
        scratch_shapes=[pltpu.VMEM((3, *before.shape), jnp.float32)],
        compiler_params=params(2),
        cost_estimate=cost(2**21, 2**22, 2**16),
        name=name,
    )(table, before, brick, *start)


def per_device(sizes, density, extinction, sun_colour, sky_colour):
    full_x, full_y = sizes
    nx, ny, nz = density.shape
    tiles = nz // LANES
    swap = functools.partial(lax.ppermute, axis_name="depth", perm=[(0, 1), (1, 0)])
    deal = functools.partial(lax.all_to_all, axis_name="light", split_axis=0, concat_axis=0, tiled=True)
    column_light, column_view, table = load_of(density, extinction, sun_colour, sky_colour, full_x, full_y)
    own = deal(column_light.reshape(ny, tiles, LANES)).reshape(ny * tiles, LANES)
    other_view = swap(column_view)
    transmittance, background = sky_of(column_view, other_view, table)
    brick, done = brick_light_of(density, other_view, table)
    before = deal(before_of(own, tiles, (done, background)).reshape(ny, tiles, LANES)).reshape(ny * tiles, LANES)
    sent = pixels_of(False, brick, before, table, "pixels_sent")
    received = swap(sent)
    kept = pixels_of(True, brick, before, table, "pixels_kept", background)
    return kept + received, transmittance


def solution(mesh):
    light = mesh.shape["light"]
    depth = mesh.shape["depth"]

    def render(density, extinction, sun_colour, sky_colour):
        full_x, full_y, _ = density.shape
        return jax.shard_map(
            functools.partial(per_device, (full_x, full_y)),
            mesh=mesh,
            in_specs=(P("light", "depth", "tile"), P(), P(), P()),
            out_specs=(P(None, ("light", "depth"), "tile"), P(None, ("light", "depth"), "tile")),
            check_vma=False,
        )(density, extinction, sun_colour, sky_colour)

    assert light == 64 and depth == 2
    return render
```

time: 269 us -> 65.8 us (0.24)
  waiting for transfers between devices: 153 us -> 0.91 us
  other arithmetic: 89.2 us -> 0.66 us
  blocking collectives: 4.96 us -> 23.5 us
  starting transfers between devices: 0.12 us -> 18.4 us
  between operations: 17.4 us -> 0.67 us
  Pallas kernels: 0 us -> 16.7 us
  local copies, waits for them, and re-layouts: 1.23 us -> 4.58 us
    all_gather x1 -> x0, waiting for transfers between devices: 139 us -> none  [prefix(): everything = lax.all_gather(value, axis)]
    select_n x66 -> x0, other arithmetic: 61.4 us -> none  [hop(): return jnp.where(reached, new, before)]
    all_to_all x0 -> x1, blocking collectives: none -> 23.5 us  [per_device(): deal(before_of(own, tiles, (done, background)).reshape(ny, tiles, LANES))]
    another operation x3 -> x0, other arithmetic: 22.5 us -> none  [the longest x1 17.3 us: per_device(): local_view = (jnp.cumsum(density, axis=1) - density) / full_y]
    pallas_call x0 -> x6, Pallas kernels: none -> 16.7 us  [the longest x1 10.6 us: brick_light_of(): pl.pallas_call(functools.partial(brick_kernel, nx, ny), grid=(nz // LANES...]
    all_to_all x0 -> x1, starting transfers between devices: none -> 15.1 us  [per_device(): deal(column_light.reshape(ny, tiles, LANES)).reshape(ny * tiles, LANES)]
    reduce_scatter x2 -> x0, waiting for transfers between devices: 13 us -> none  [the longest x1 12.9 us: per_device(): lax.psum_scatter(contribution, 'depth', scatter_dimension=1, tiled=True)]
    all_gather x1 -> x0, blocking collectives: 4.96 us -> none  [prefix(): everything = lax.all_gather(value, axis)]
  transfers between devices with their start and end apart: 3 -> 3, of which waited for: 2 -> 1; matrix products, arithmetic and copies ran while one was open for 32% -> 0% of each run, Pallas kernels for 0% -> 19%
where the time goes in v2:
time: 65.8 us; the launch traced here: 65.5 us
  blocking collectives  23.5 us (36%)
  starting transfers between devices  18.4 us (28%)
  Pallas kernels  16.7 us (25%)
  local copies, waits for them, and re-layouts  4.58 us (7%)
  waiting for transfers between devices  0.91 us (1%)
  between operations  0.67 us (1%)
  other arithmetic  0.66 us (1%)
    all_to_all x1, blocking collectives, per_device(): deal(before_of(own, tiles, (done, background)).reshape(ny, tiles, LANES))  23.5 us
    all_to_all x1, starting transfers between devices, per_device(): deal(column_light.reshape(ny, tiles, LANES)).reshape(ny * tiles, LANES)  15.1 us
    pallas_call x1, Pallas kernels, brick_light_of(): pl.pallas_call(functools.partial(brick_kernel, nx, ny), grid=(nz // LANES...  10.6 us
    unnamed x2, local copies, waits for them, and re-layouts  4.58 us
    pallas_call x1, Pallas kernels, load_of(): pl.pallas_call(functools.partial(load_kernel, (nx, ny, full_x, full_y)),...  3.3 us
    ppermute x1, starting transfers between devices, per_device(): received = swap(sent)  2.24 us
    pallas_call x2, Pallas kernels, pixels_of(): pl.pallas_call(functools.partial(pixel_kernel, own), in_specs=[VMEM] * (3...  2.14 us
  transfers between devices with their start and end apart: 3, of which 1 were waited for; matrix products, arithmetic and copies ran while one was open for 0% of the time, Pallas kernels for 19%

profile of v2, /device:TPU:1, one launch (start us, length us, event | category | flops | bytes accessed | tf_op | source)
XLA Modules:
  0.0 65.5 jit_solution(16807017272434343182)
XLA Ops:
  0.6 3.3 %load.1 = (f32[256,128]{1,0:T(8,128)}, f32[32,512]{1,0:T(8,128)S(1)}, f32[96,128]{1,0:T(8,128)S(1)}) custom-call(f32[2048,512]{1,0:T(8,128)} %bitcast.9, f32[3]{0:T(128)} %ext_ref.1, f32[3]{0:T(128)} %sun_ref.1, f32[3]{0:T(128)} %sky_ref.1), custom_call_target="tpu_custom_call" | custom-call | flops 2097152 | bytes 8388608 | tf_op jit(solution)/shard_map/load/pallas_call | solution.py:73
  3.9 15.1 %all-to-all-start = ((f32[64,4,128]{2,1,0:T(4,128)}), f32[64,4,128]{2,1,0:T(4,128)S(1)}, u32[]{:S(2)}, u32[]{:S(2)}) async-start(f32[64,4,128]{2,1,0:T(4,128)} %bitcast.1), calls=%async_computation | async-start | bytes 262144 | tf_op jit(solution)/shard_map/all_to_all | solution.py:256
  19.1 1.0 %collective-permute-start = (f32[32,512]{1,0:T(8,128)S(1)}, f32[32,512]{1,0:T(8,128)S(1)}, u32[]{:S(2)}, u32[]{:S(2)}) collective-permute-start(f32[32,512]{1,0:T(8,128)S(1)} %get-tuple-element.11.view_ref), channel_id=1, source_target_pairs={{0,2},{2,0},{1,3},{3,1},{4,6},{6,4},{5,7},{7,5},{8,10},{10,8},{9,1... | collective-permute-start | bytes 196616 | tf_op jit(solution)/shard_map/ppermute | solution.py:257
  20.1 0.9 %collective-permute-done.other_ref = f32[32,512]{1,0:T(8,128)S(1)} collective-permute-done((f32[32,512]{1,0:T(8,128)S(1)}, f32[32,512]{1,0:T(8,128)S(1)}, u32[]{:S(2)}, u32[]{:S(2)}) %collective-permute-start) | collective-permute-done | bytes 65568 | tf_op jit(solution)/shard_map/ppermute | solution.py:257
  21.0 0.7 %sky.1 = (f32[3,16,512]{2,1,0:T(8,128)}, f32[3,16,512]{2,1,0:T(8,128)S(1)}) custom-call(f32[96,128]{1,0:T(8,128)S(1)} %get-tuple-element.9.table_ref, f32[32,512]{1,0:T(8,128)S(1)} %get-tuple-element.11.view_ref, f32[32,512]{1,0:T(8,128)S(1)} %collective-permute-done.other_ref), custom_call_target="tpu_custom_call" | custom-call | tf_op jit(solution)/shard_map/sky/pallas_call | solution.py:199
  21.7 10.6 %brick_light.1 = (f32[4,3,64,32,128]{4,3,2,1,0:T(8,128)}, f32[8,128]{1,0:T(8,128)S(1)}) custom-call(f32[96,128]{1,0:T(8,128)S(1)} %get-tuple-element.9.table_ref, f32[32,512]{1,0:T(8,128)S(1)} %collective-permute-done.other_ref, f32[2048,512]{1,0:T(8,128)} %bitcast.10), custom_call_target="tpu_custom_call" | custom-call | flops 33554432 | bytes 16777216 | tf_op jit(solution)/shard_map/brick_light/pallas_call | solution.py:163
  32.3 0.0 all-to-all-done
  32.3 23.5 %all_to_all.10 = f32[64,4,128]{2,1,0:T(4,128)S(1)} all-to-all(f32[64,4,128]{2,1,0:T(4,128)S(1)} %bitcast.8), channel_id=1, replica_groups=mesh['light'=64,'depth'=2,'tile'=2] {'light'}, dimensions={0} | all-to-all | bytes 262144 | tf_op jit(solution)/shard_map/all_to_all | solution.py:260
  55.9 0.0 copy-start
  55.9 4.6 %copy-done = f32[4,3,64,32,128]{4,3,2,1,0:T(8,128)S(1)} copy-done((f32[4,3,64,32,128]{4,3,2,1,0:T(8,128)S(1)}, f32[4,3,64,32,128]{4,3,2,1,0:T(8,128)}, u32[]{:S(2)}) %copy-start) | copy-done | bytes 12582936
  60.4 1.0 %pixels_sent.1 = f32[3,16,512]{2,1,0:T(8,128)S(1)} custom-call(f32[96,128]{1,0:T(8,128)S(1)} %get-tuple-element.9.table_ref, f32[256,128]{1,0:T(8,128)S(1)} %bitcast.5, f32[4,3,64,32,128]{4,3,2,1,0:T(8,128)S(1)} %copy-done), custom_call_target="tpu_custom_call" | custom-call | flops 2097152 | bytes 4194304 | tf_op jit(solution)/shard_map/pixels_sent/pallas_call | solution.py:237
  61.4 2.2 %collective-permute-start.1 = (f32[3,16,512]{2,1,0:T(8,128)S(1)}, f32[3,16,512]{2,1,0:T(8,128)S(1)}, u32[]{:S(2)}, u32[]{:S(2)}) collective-permute-start(f32[3,16,512]{2,1,0:T(8,128)S(1)} %pixels_sent.1), channel_id=1, source_target_pairs={{0,2},{2,0},{1,3},{3,1},{4,6},{6,4},{5,7},{7,5},{8,10},{10,8},{9,1... | collective-permute-start | bytes 294920 | tf_op jit(solution)/shard_map/ppermute | solution.py:262
  63.7 1.1 %pixels_kept.1 = f32[3,16,512]{2,1,0:T(8,128)S(1)} custom-call(f32[96,128]{1,0:T(8,128)S(1)} %get-tuple-element.9.table_ref, f32[256,128]{1,0:T(8,128)S(1)} %bitcast.6, f32[4,3,64,32,128]{4,3,2,1,0:T(8,128)S(1)} %copy-done, f32[3,16,512]{2,1,0:T(8,128)S(1)} %get-tuple-element.13.refs_1_), custom_call_target="tpu_custom_call" | custom-call | flops 2097152 | bytes 4194304 | tf_op jit(solution)/shard_map/pixels_kept/pallas_call | solution.py:237
  64.8 0.0 collective-permute-done.1
  64.8 0.7 %add.3 = f32[3,16,512]{2,1,0:T(8,128)} add(f32[3,16,512]{2,1,0:T(8,128)S(1)} %pixels_kept.1, f32[3,16,512]{2,1,0:T(8,128)S(1)} %collective-permute-done.1) | non-fusion elementwise | flops 24576 | bytes 294912 | tf_op jit(solution)/shard_map/add | solution.py:264
  (1 shorter events, 0.0 us)
Async XLA Ops:
  3.9 28.3 %all-to-all-start = ((f32[64,4,128]{2,1,0:T(4,128)}), f32[64,4,128]{2,1,0:T(4,128)S(1)}, u32[]{:S(2)}, u32[]{:S(2)}) async-start(f32[64,4,128]{2,1,0:T(4,128)} %bitcast.1), calls=%async_computation | async-start | bytes 262144 | tf_op jit(solution)/shard_map/all_to_all | solution.py:256
  19.1 1.9 %collective-permute-start = (f32[32,512]{1,0:T(8,128)S(1)}, f32[32,512]{1,0:T(8,128)S(1)}, u32[]{:S(2)}, u32[]{:S(2)}) collective-permute-start(f32[32,512]{1,0:T(8,128)S(1)} %get-tuple-element.11.view_ref), channel_id=1, source_target_pairs={{0,2},{2,0},{1,3},{3,1},{4,6},{6,4},{5,7},{7,5},{8,10},{10,8},{9,1... | collective-permute-start | bytes 196616 | tf_op jit(solution)/shard_map/ppermute | solution.py:257
  55.9 4.6 %copy-start = (f32[4,3,64,32,128]{4,3,2,1,0:T(8,128)S(1)}, f32[4,3,64,32,128]{4,3,2,1,0:T(8,128)}, u32[]{:S(2)}) copy-start(f32[4,3,64,32,128]{4,3,2,1,0:T(8,128)} %get-tuple-element.14.refs_0_) | copy-start | bytes 37748740
  61.4 3.4 %collective-permute-start.1 = (f32[3,16,512]{2,1,0:T(8,128)S(1)}, f32[3,16,512]{2,1,0:T(8,128)S(1)}, u32[]{:S(2)}, u32[]{:S(2)}) collective-permute-start(f32[3,16,512]{2,1,0:T(8,128)S(1)} %pixels_sent.1), channel_id=1, source_target_pairs={{0,2},{2,0},{1,3},{3,1},{4,6},{6,4},{5,7},{7,5},{8,10},{10,8},{9,1... | collective-permute-start | bytes 294920 | tf_op jit(solution)/shard_map/ppermute | solution.py:262

commit v3 on v0

v3 whole, which is shorter than its diff:
```python
import functools

import jax
import jax.numpy as jnp
from jax import lax
from jax.experimental import pallas as pl
from jax.experimental.pallas import tpu as pltpu
from jax.sharding import Mesh
from jax.sharding import PartitionSpec as P

LANES = 128
CHUNKS = 8
PIECES = 2
LOG2E = 1.4426950408889634
VMEM = pl.BlockSpec(memory_space=pltpu.VMEM)
HBM = pl.BlockSpec(memory_space=pltpu.HBM)
PLANE = ("y", "x")


def params(mib):
    return pltpu.CompilerParams(vmem_limit_bytes=mib * 1024 * 1024)


def cost(flops, size, transcendentals=0):
    return pl.CostEstimate(flops=flops, bytes_accessed=size, transcendentals=transcendentals)


def in_hbm(*arrays):
    return [pltpu.with_memory_space_constraint(x, pltpu.HBM) for x in arrays]


def load_kernel(sizes, density_ref, ext_ref, sun_ref, sky_ref, light_ref, table_ref, held_ref, three_ref, sems, small_sems):
    nx, full_x, full_y = sizes
    planes = nx // CHUNKS
    copies = [
        pltpu.make_async_copy(density_ref.at[pl.ds(k * planes, planes)], held_ref.at[pl.ds(k * planes, planes)], sems.at[k])
        for k in range(CHUNKS)
    ]
    small = [
        pltpu.make_async_copy(source, three_ref.at[i], small_sems.at[i]) for i, source in enumerate((ext_ref, sun_ref, sky_ref))
    ]
    for copy in (*copies, *small):
        copy.start()
    for k in range(CHUNKS):
        copies[k].wait()
        part = held_ref[k * planes]
        for x in range(k * planes + 1, (k + 1) * planes):
            part = part + held_ref[x]
        light_ref[...] = part if k == 0 else light_ref[...] + part
    for copy in small:
        copy.wait()
    for c in range(3):
        row = (-LOG2E / full_y * three_ref[0, c], -LOG2E / full_x * three_ref[0, c], three_ref[1, c], three_ref[2, c])
        for i, value in enumerate(row):
            table_ref[8 * (4 * c + i) : 8 * (4 * c + i) + 8] = jnp.full((8, LANES), value, jnp.float32)


def factor(table_ref, c, which):
    return table_ref[8 * (4 * c + which) : 8 * (4 * c + which) + 8]


def load_of(density, extinction, sun_colour, sky_colour, full_x, full_y):
    nx, ny, nz = density.shape
    return pl.pallas_call(
        functools.partial(load_kernel, (nx, full_x, full_y)),
        in_specs=[HBM, HBM, HBM, HBM],
        out_specs=[VMEM, VMEM],
        out_shape=[
            jax.ShapeDtypeStruct((ny, nz), jnp.float32),
            jax.ShapeDtypeStruct((12 * 8, LANES), jnp.float32),
        ],
        scratch_shapes=[
            pltpu.VMEM((nx, ny, nz), jnp.float32),
            pltpu.SMEM((3, 3), jnp.float32),
            pltpu.SemaphoreType.DMA((CHUNKS,)),
            pltpu.SemaphoreType.DMA((3,)),
        ],
        compiler_params=params(8),
        cost_estimate=cost(2**21, 2**23),
        name="load",
    )(*in_hbm(density, extinction, sun_colour, sky_colour))


def plane_kernel(own_ref, *refs):
    within_ref, sums_ref = refs[-2], refs[-1]
    members, part, _ = own_ref.shape
    total = jnp.zeros_like(own_ref[0])
    for k in range(members):
        within_ref[k] = total
        total = total + own_ref[k]
    for k in range(sums_ref.shape[0]):
        sums_ref[k] = total


def plane_of(own, planes, after):
    members, part, nz = own.shape
    return pl.pallas_call(
        plane_kernel,
        in_specs=[VMEM] * (1 + len(after)),
        out_specs=[VMEM, VMEM],
        out_shape=[jax.ShapeDtypeStruct(own.shape, jnp.float32), jax.ShapeDtypeStruct((planes, part, nz), jnp.float32)],
        compiler_params=params(2),
        name="plane_sums",
    )(own, *after)


def nearer_kernel(sums_ref, within_ref, *refs):
    back_ref = refs[-1]
    plane = lax.axis_index("z")
    total = jnp.zeros_like(sums_ref[0])
    for k in range(sums_ref.shape[0] - 1):
        total = total + sums_ref[k] * (k < plane).astype(jnp.float32)
    for k in range(within_ref.shape[0]):
        back_ref[k] = within_ref[k] + total


def nearer_of(sums, within, after):
    return pl.pallas_call(
        nearer_kernel,
        in_specs=[VMEM] * (2 + len(after)),
        out_specs=VMEM,
        out_shape=jax.ShapeDtypeStruct(within.shape, jnp.float32),
        compiler_params=params(2),
        name="nearer",
    )(sums, within, *after)


def brick_kernel(nx, ny, table_ref, d_ref, sent_ref, kept_ref, view_ref, done_ref, s_ref):
    own = lax.axis_index("depth")
    rows = nx // 2
    wide = 32
    done_ref[...] = jnp.zeros_like(done_ref)

    def along_x(part, _):
        carry = jnp.zeros((wide, LANES), jnp.float32)
        for x in range(nx):
            at = pl.ds(pl.multiple_of(x * ny + part * wide, 8), wide)
            cell = d_ref[at, :]
            s_ref[at, :] = carry + 0.5 * cell
            carry = carry + cell
        return 0

    lax.fori_loop(0, ny // wide, along_x, 0)
    view_rate = [factor(table_ref, c, 0) for c in range(3)]
    sun_rate = [factor(table_ref, c, 1) for c in range(3)]
    for out_ref, half in ((sent_ref, 1 - own), (kept_ref, own)):
        start = half * rows

        def cells(step, state, out_ref=out_ref, start=start):
            view, passing = list(state[0]), [list(p) for p in state[1]]
            for k in range(8):
                y = step * 8 + k
                light = [[None, None] for _ in range(3)]
                for t in range(2):
                    at = pl.ds((start + 8 * t) * ny + y, 8, stride=ny)
                    view[t] = view[t] + d_ref[at, :]
                    sun = s_ref[at, :]
                    for c in range(3):
                        later = jnp.exp2(view[t] * view_rate[c])
                        light[c][t] = (passing[c][t] - later) * jnp.exp2(sun * sun_rate[c])
                        passing[c][t] = later
                for c in range(3):
                    out_ref[0, c, y] = jnp.concatenate(light[c], axis=0).astype(out_ref.dtype)
            return tuple(view), tuple(tuple(p) for p in passing)

        zero, one = jnp.zeros((8, LANES), jnp.float32), jnp.ones((8, LANES), jnp.float32)
        view, _ = lax.fori_loop(0, ny // 8, cells, ((zero, zero), ((one, one),) * 3))
        for t in range(2):
            view_ref[pl.ds(pl.multiple_of(start + 8 * t, 8), 8), :] = view[t]


def brick_light_of(density, table, piece, after):
    nx, ny, nz = density.shape
    tiles = nz // LANES // PIECES
    light = pltpu.HBM((tiles, 3, ny, nx // 2, LANES), jnp.bfloat16)
    spec = pl.BlockSpec((1, 3, ny, nx // 2, LANES), lambda i: (i, 0, 0, 0, 0))
    ignore = len(after)

    def kernel(table_ref, d_ref, *refs):
        brick_kernel(nx, ny, table_ref, d_ref, *refs[ignore:])

    return pl.pallas_call(
        kernel,
        grid=(tiles,),
        in_specs=[VMEM, pl.BlockSpec((nx * ny, LANES), lambda i: (0, piece * tiles + i)), *[HBM] * ignore],
        out_specs=[spec, spec, pl.BlockSpec((nx, LANES), lambda i: (0, i)), VMEM],
        out_shape=[
            light,
            light,
            jax.ShapeDtypeStruct((nx, tiles * LANES), jnp.float32),
            jax.ShapeDtypeStruct((8, LANES), jnp.float32),
        ],
        scratch_shapes=[pltpu.VMEM((nx * ny, LANES), jnp.float32)],
        compiler_params=params(8),
        cost_estimate=cost(2**24, 2**23, 3 * 2**20),
        name=f"brick_light_{piece}",
    )(table, *in_hbm(density.reshape(nx * ny, nz), *after))


def sky_kernel(table_ref, *refs):
    passed_ref, behind_ref, front_ref = refs[-3:]
    views, others = refs[:PIECES], refs[PIECES : 2 * PIECES]
    _, rows, nz = passed_ref.shape
    own = lax.axis_index("depth")
    far = own.astype(jnp.float32)
    for lane in range(0, nz, LANES):
        piece, inner = divmod(lane, nz // PIECES)
        lanes, at = slice(lane, lane + LANES), slice(inner, inner + LANES)
        for row in range(0, rows, 8):
            mine = pl.ds(pl.multiple_of(own * rows + row, 8), 8)
            column = views[piece][mine, at] + others[piece][mine, at]
            for c in range(3):
                passed = jnp.exp2(column * factor(table_ref, c, 0))
                passed_ref[c, row : row + 8, lanes] = passed
                behind_ref[c, row : row + 8, lanes] = factor(table_ref, c, 3) * passed
        for j, half in enumerate((1 - own, own)):
            for row in range(0, rows, 8):
                mine = pl.ds(pl.multiple_of(half * rows + row, 8), 8)
                for c in range(3):
                    front_ref[j, c, row : row + 8, lanes] = jnp.exp2(others[piece][mine, at] * far * factor(table_ref, c, 0))


def sky_of(table, views, others):
    nx, width = views[0].shape
    shape = jax.ShapeDtypeStruct((3, nx // 2, width * PIECES), jnp.float32)
    return pl.pallas_call(
        sky_kernel,
        in_specs=[VMEM] * (1 + 2 * PIECES),
        out_specs=[VMEM, VMEM, VMEM],
        out_shape=[shape, shape, jax.ShapeDtypeStruct((2, *shape.shape), jnp.float32)],
        compiler_params=params(4),
        cost_estimate=cost(2**17, 2**20, 2**17),
        name="sky",
    )(table, *views, *others)


def pixel_kernel(own, table_ref, before_ref, front_ref, *refs):
    lights, start_ref, out_ref, a_ref, held_ref, sems = refs[:PIECES], refs[PIECES:-4], refs[-4], refs[-3], refs[-2], refs[-1]
    tiles, _, ny, rows, _ = lights[0].shape
    copies = [
        pltpu.make_async_copy(lights[piece].at[t, c], held_ref.at[piece * tiles + t, c], sems.at[piece * tiles + t, c])
        for piece in range(PIECES)
        for t in range(tiles)
        for c in range(3)
    ]
    for copy in copies:
        copy.start()
    for c in range(3):
        rate, colour = factor(table_ref, c, 1)[:1], factor(table_ref, c, 2)[:1]
        for t in range(tiles * PIECES):
            lanes = slice(t * LANES, (t + 1) * LANES)
            a_ref[c, :, lanes] = colour * jnp.exp2(before_ref[:, lanes] * rate)
    ways = 4
    for t in range(tiles * PIECES):
        lanes = slice(t * LANES, (t + 1) * LANES)
        for c in range(3):
            copies[3 * t + c].wait()
            total = [jnp.zeros((rows, LANES), jnp.float32) for _ in range(ways)]
            for y in range(ny):
                light = jnp.broadcast_to(a_ref[c, y : y + 1, lanes], (rows, LANES))
                total[y % ways] = total[y % ways] + light * held_ref[t, c, y].astype(jnp.float32)
            value = ((total[0] + total[1]) + (total[2] + total[3])) * front_ref[int(own), c, :, lanes]
            out_ref[c, :, lanes] = value + start_ref[0][c, :, lanes] if start_ref else value


def pixels_of(own, lights, before, front, table, name, *start):
    tiles, _, ny, rows, _ = lights[0].shape
    ny, nz = before.shape
    return pl.pallas_call(
        functools.partial(pixel_kernel, own),
        in_specs=[VMEM] * 3 + [HBM] * PIECES + [VMEM] * len(start),
        out_specs=VMEM,
        out_shape=jax.ShapeDtypeStruct((3, rows, nz), jnp.float32),
        scratch_shapes=[
            pltpu.VMEM((3, ny, nz), jnp.float32),
            pltpu.VMEM((tiles * PIECES, 3, ny, rows, LANES), jnp.bfloat16),
            pltpu.SemaphoreType.DMA((tiles * PIECES, 3)),
        ],
        compiler_params=params(8),
        cost_estimate=cost(2**21, 2**22, 2**16),
        name=name,
    )(table, before, front, *in_hbm(*lights), *start)


def per_device(sizes, density, extinction, sun_colour, sky_colour):
    planes, members, full_x, full_y = sizes
    nx, ny, nz = density.shape
    part = ny // members
    swap = functools.partial(lax.ppermute, axis_name="depth", perm=[(0, 1), (1, 0)])
    deal = functools.partial(lax.all_to_all, split_axis=0, concat_axis=0, tiled=True)
    column_light, table = load_of(density, extinction, sun_colour, sky_colour, full_x, full_y)
    own = deal(column_light.reshape(members, part, nz), PLANE)
    sent0, kept0, view0, done0 = brick_light_of(density, table, 0, ())
    within, sums = plane_of(own, planes, (done0,))
    sums = deal(sums, "z")
    sent1, kept1, view1, done1 = brick_light_of(density, table, 1, ())
    back = nearer_of(sums, within, (done1,))
    before = deal(back, PLANE).reshape(ny, nz)
    views = (view0, view1)
    transmittance, background, front = sky_of(table, views, [swap(view) for view in views])
    sent = pixels_of(False, (sent0, sent1), before, front, table, "pixels_sent")
    received = swap(sent)
    kept = pixels_of(True, (kept0, kept1), before, front, table, "pixels_kept", background)
    return kept + received, transmittance


def solution(mesh):
    shape = (8, 4, 2, 2, 2)
    fine = Mesh(mesh.devices.reshape(shape), ("z", *PLANE, "depth", "tile"))
    light = ("z", *PLANE)
    sizes = (8, 8, 2048, 128)
    return jax.shard_map(
        functools.partial(per_device, sizes),
        mesh=fine,
        in_specs=(P(light, "depth", "tile"), P(), P(), P()),
        out_specs=(P(None, (*light, "depth"), "tile"), P(None, (*light, "depth"), "tile")),
        check_vma=False,
    )
```

time: 269 us -> 57.3 us (0.21)
  waiting for transfers between devices: 153 us -> 7 us
  other arithmetic: 89.2 us -> 0.66 us
  starting transfers between devices: 0.12 us -> 28.1 us
  Pallas kernels: 0 us -> 20.4 us
  between operations: 17.4 us -> 0.67 us
  blocking collectives: 4.96 us -> 0 us
    all_gather x1 -> x0, waiting for transfers between devices: 139 us -> none  [prefix(): everything = lax.all_gather(value, axis)]
    select_n x66 -> x0, other arithmetic: 61.4 us -> none  [hop(): return jnp.where(reached, new, before)]
    another operation x3 -> x0, other arithmetic: 22.5 us -> none  [the longest x1 17.3 us: per_device(): local_view = (jnp.cumsum(density, axis=1) - density) / full_y]
    all_to_all x0 -> x3, starting transfers between devices: none -> 20.9 us  [the longest x1 8.19 us: per_device(): sums = deal(sums, 'z')]
    pallas_call x0 -> x8, Pallas kernels: none -> 20.4 us  [the longest x2 11.5 us: brick_light_of(): pl.pallas_call(kernel, grid=(tiles,), in_specs=[VMEM, pl.BlockSpec((nx *...]
    reduce_scatter x2 -> x0, waiting for transfers between devices: 13 us -> none  [the longest x1 12.9 us: per_device(): lax.psum_scatter(contribution, 'depth', scatter_dimension=1, tiled=True)]
    ppermute x0 -> x3, starting transfers between devices: none -> 7.16 us  [the longest x1 4.15 us: per_device(): received = swap(sent)]
    all_to_all x0 -> x3, waiting for transfers between devices: none -> 5.89 us  [the longest x1 2.31 us: per_device(): sums = deal(sums, 'z')]
  transfers between devices with their start and end apart: 3 -> 6, of which waited for: 2 -> 5; matrix products, arithmetic and copies ran while one was open for 32% -> 0% of each run, Pallas kernels for 0% -> 25%
where the time goes in v3:
time: 57.3 us; the launch traced here: 56.8 us
  starting transfers between devices  28.1 us (49%)
  Pallas kernels  20.4 us (36%)
  waiting for transfers between devices  7 us (12%)
  between operations  0.67 us (1%)
  other arithmetic  0.66 us (1%)
    pallas_call x2, Pallas kernels, brick_light_of(): pl.pallas_call(kernel, grid=(tiles,), in_specs=[VMEM, pl.BlockSpec((nx *...  11.5 us
    all_to_all x1, starting transfers between devices, per_device(): sums = deal(sums, 'z')  8.19 us
    all_to_all x1, starting transfers between devices, per_device(): own = deal(column_light.reshape(members, part, nz), PLANE)  7.49 us
    all_to_all x1, starting transfers between devices, per_device(): before = deal(back, PLANE).reshape(ny, nz)  5.26 us
    ppermute x1, starting transfers between devices, per_device(): received = swap(sent)  4.15 us
    pallas_call x2, Pallas kernels, pixels_of(): pl.pallas_call(functools.partial(pixel_kernel, own), in_specs=[VMEM] * 3...  3.96 us
    ppermute x2, starting transfers between devices, per_device(): swap(view)  3.01 us
    pallas_call x1, Pallas kernels, load_of(): pl.pallas_call(functools.partial(load_kernel, (nx, full_x, full_y)), in_s...  2.96 us
  transfers between devices with their start and end apart: 6, of which 5 were waited for; matrix products, arithmetic and copies ran while one was open for 0% of the time, Pallas kernels for 25%

profile of v3, /device:TPU:1, one launch (start us, length us, event | category | flops | bytes accessed | tf_op | source)
XLA Modules:
  0.0 56.8 jit_solution(18382197992398127822)
XLA Ops:
  0.6 3.0 %load.1 = (f32[64,512]{1,0:T(8,128)}, f32[96,128]{1,0:T(8,128)S(1)}) custom-call(f32[32,64,512]{2,1,0:T(8,128)} %density_ref.1, f32[3]{0:T(128)} %ext_ref.1, f32[3]{0:T(128)} %sun_ref.1, f32[3]{0:T(128)} %sky_ref.1), custom_call_target="tpu_custom_call" | custom-call | flops 2097152 | bytes 8388608 | tf_op jit(solution)/shard_map/load/pallas_call | solution.py:64
  3.6 7.5 %all-to-all-start = ((f32[8,8,512]{2,1,0:T(8,128)}), f32[8,8,512]{2,1,0:T(8,128)S(1)}, u32[]{:S(2)}, u32[]{:S(2)}) async-start(f32[8,8,512]{2,1,0:T(8,128)} %bitcast), calls=%async_computation | async-start | bytes 262144 | tf_op jit(solution)/shard_map/all_to_all | solution.py:292
  11.1 5.7 %brick_light_0.1 = (bf16[2,3,64,16,128]{4,3,2,1,0:T(8,128)(2,1)}, bf16[2,3,64,16,128]{4,3,2,1,0:T(8,128)(2,1)}, f32[32,256]{1,0:T(8,128)S(1)}, f32[8,128]{1,0:T(8,128)S(1)}) custom-call(f32[96,128]{1,0:T(8,128)S(1)} %get-tuple-element.17.table_ref, f32[2048,512]{1,0:T(8,128)} %bitcast.5), custom_call_target="tpu_custom_call" | custom-call | flops 16777216 | bytes 8388608 | tf_op jit(solution)/shard_map/brick_light_0/pallas_call | solution.py:182
  16.8 1.3 %all-to-all-done.own_ref = f32[8,8,512]{2,1,0:T(8,128)S(1)} async-done(((f32[8,8,512]{2,1,0:T(8,128)}), f32[8,8,512]{2,1,0:T(8,128)S(1)}, u32[]{:S(2)}, u32[]{:S(2)}) %all-to-all-start) | async-done | bytes 131104 | tf_op jit(solution)/shard_map/all_to_all | solution.py:292
  18.1 0.7 %plane_sums.1 = (f32[8,8,512]{2,1,0:T(8,128)S(1)}, f32[8,8,512]{2,1,0:T(8,128)}) custom-call(f32[8,8,512]{2,1,0:T(8,128)S(1)} %all-to-all-done.own_ref, f32[8,128]{1,0:T(8,128)S(1)} %get-tuple-element.19.refs_0_), custom_call_target="tpu_custom_call" | custom-call | tf_op jit(solution)/shard_map/plane_sums/pallas_call | solution.py:97
  18.8 8.2 %all-to-all-start.1 = ((f32[8,8,512]{2,1,0:T(8,128)}), f32[8,8,512]{2,1,0:T(8,128)S(1)}, u32[]{:S(2)}, u32[]{:S(2)}) async-start(f32[8,8,512]{2,1,0:T(8,128)} %get-tuple-element.20), calls=%async_computation.1 | async-start | bytes 262144 | tf_op jit(solution)/shard_map/all_to_all | solution.py:295
  27.0 5.7 %brick_light_1.1 = (bf16[2,3,64,16,128]{4,3,2,1,0:T(8,128)(2,1)}, bf16[2,3,64,16,128]{4,3,2,1,0:T(8,128)(2,1)}, f32[32,256]{1,0:T(8,128)S(1)}, f32[8,128]{1,0:T(8,128)S(1)}) custom-call(f32[96,128]{1,0:T(8,128)S(1)} %get-tuple-element.17.table_ref, f32[2048,512]{1,0:T(8,128)} %bitcast.6), custom_call_target="tpu_custom_call" | custom-call | flops 16777216 | bytes 8388608 | tf_op jit(solution)/shard_map/brick_light_1/pallas_call | solution.py:182
  32.7 2.3 %all-to-all-done.1.sums_ref = f32[8,8,512]{2,1,0:T(8,128)S(1)} async-done(((f32[8,8,512]{2,1,0:T(8,128)}), f32[8,8,512]{2,1,0:T(8,128)S(1)}, u32[]{:S(2)}, u32[]{:S(2)}) %all-to-all-start.1) | async-done | bytes 131104 | tf_op jit(solution)/shard_map/all_to_all | solution.py:295
  35.0 0.7 %nearer.1 = f32[8,8,512]{2,1,0:T(8,128)} custom-call(f32[8,8,512]{2,1,0:T(8,128)S(1)} %all-to-all-done.1.sums_ref, f32[8,8,512]{2,1,0:T(8,128)S(1)} %get-tuple-element.21.within_ref, f32[8,128]{1,0:T(8,128)S(1)} %get-tuple-element.22.refs_0_), custom_call_target="tpu_custom_call" | custom-call | tf_op jit(solution)/shard_map/nearer/pallas_call | solution.py:118
  35.7 5.3 %all-to-all-start.2 = ((f32[8,8,512]{2,1,0:T(8,128)}), f32[8,8,512]{2,1,0:T(8,128)S(1)}, u32[]{:S(2)}, u32[]{:S(2)}) async-start(f32[8,8,512]{2,1,0:T(8,128)} %nearer.1), calls=%async_computation.2 | async-start | bytes 262144 | tf_op jit(solution)/shard_map/all_to_all | solution.py:298
  40.9 2.9 %collective-permute-start.1 = (f32[32,256]{1,0:T(8,128)S(1)}, f32[32,256]{1,0:T(8,128)S(1)}, u32[]{:S(2)}, u32[]{:S(2)}) collective-permute-start(f32[32,256]{1,0:T(8,128)S(1)} %get-tuple-element.24.refs_1_), channel_id=1, source_target_pairs={{0,2},{2,0},{1,3},{3,1},{4,6},{6,4},{5,7},{7,5},{8,10},{10,8},{9,1... | collective-permute-start | bytes 98312 | tf_op jit(solution)/shard_map/ppermute | solution.py:300
  43.9 0.1 collective-permute-start
  44.0 0.8 %collective-permute-done.1.refs_3_ = f32[32,256]{1,0:T(8,128)S(1)} collective-permute-done((f32[32,256]{1,0:T(8,128)S(1)}, f32[32,256]{1,0:T(8,128)S(1)}, u32[]{:S(2)}, u32[]{:S(2)}) %collective-permute-start.1) | collective-permute-done | bytes 32800 | tf_op jit(solution)/shard_map/ppermute | solution.py:300
  44.7 0.3 collective-permute-done.refs_2_
  45.1 0.7 %sky.1 = (f32[3,16,512]{2,1,0:T(8,128)}, f32[3,16,512]{2,1,0:T(8,128)S(1)}, f32[2,3,16,512]{3,2,1,0:T(8,128)S(1)}) custom-call(f32[96,128]{1,0:T(8,128)S(1)} %get-tuple-element.17.table_ref, f32[32,256]{1,0:T(8,128)S(1)} %get-tuple-element.23.refs_0_, f32[32,256]{1,0:T(8,128)S(1)} %get-tuple-element.24.refs_1_, f32[32,256]{1,0:T(8,128)S(1)} %collective-permute-done.refs_2_, ...), custom_call_target="tpu_custom_call" | custom-call | flops 131072 | bytes 1048576 | tf_op jit(solution)/shard_map/sky/pallas_call | solution.py:226
  45.7 2.3 %all-to-all-done.2 = f32[8,8,512]{2,1,0:T(8,128)S(1)} async-done(((f32[8,8,512]{2,1,0:T(8,128)}), f32[8,8,512]{2,1,0:T(8,128)S(1)}, u32[]{:S(2)}, u32[]{:S(2)}) %all-to-all-start.2) | async-done | bytes 131104 | tf_op jit(solution)/shard_map/all_to_all | solution.py:298
  48.0 2.0 %pixels_sent.1 = f32[3,16,512]{2,1,0:T(8,128)S(1)} custom-call(f32[96,128]{1,0:T(8,128)S(1)} %get-tuple-element.17.table_ref, f32[64,512]{1,0:T(8,128)S(1)} %bitcast.3, f32[2,3,16,512]{3,2,1,0:T(8,128)S(1)} %get-tuple-element.25.front_ref, bf16[2,3,64,16,128]{4,3,2,1,0:T(8,128)(2,1)} %get-tuple-element.29.refs_0_, ...), custom_call_target="tpu_custom_call" | custom-call | flops 2097152 | bytes 4194304 | tf_op jit(solution)/shard_map/pixels_sent/pallas_call | solution.py:269
  50.0 4.1 %collective-permute-start.2 = (f32[3,16,512]{2,1,0:T(8,128)S(1)}, f32[3,16,512]{2,1,0:T(8,128)S(1)}, u32[]{:S(2)}, u32[]{:S(2)}) collective-permute-start(f32[3,16,512]{2,1,0:T(8,128)S(1)} %pixels_sent.1), channel_id=1, source_target_pairs={{0,2},{2,0},{1,3},{3,1},{4,6},{6,4},{5,7},{7,5},{8,10},{10,8},{9,1... | collective-permute-start | bytes 294920 | tf_op jit(solution)/shard_map/ppermute | solution.py:302
  54.1 2.0 %pixels_kept.1 = f32[3,16,512]{2,1,0:T(8,128)S(1)} custom-call(f32[96,128]{1,0:T(8,128)S(1)} %get-tuple-element.17.table_ref, f32[64,512]{1,0:T(8,128)S(1)} %bitcast.4, f32[2,3,16,512]{3,2,1,0:T(8,128)S(1)} %get-tuple-element.25.front_ref, bf16[2,3,64,16,128]{4,3,2,1,0:T(8,128)(2,1)} %get-tuple-element.26.refs_0_, ...), custom_call_target="tpu_custom_call" | custom-call | flops 2097152 | bytes 4194304 | tf_op jit(solution)/shard_map/pixels_kept/pallas_call | solution.py:269
  56.1 0.0 collective-permute-done.2
  56.1 0.7 %add.3 = f32[3,16,512]{2,1,0:T(8,128)} add(f32[3,16,512]{2,1,0:T(8,128)S(1)} %pixels_kept.1, f32[3,16,512]{2,1,0:T(8,128)S(1)} %collective-permute-done.2) | non-fusion elementwise | flops 24576 | bytes 294912 | tf_op jit(solution)/shard_map/add | solution.py:304
Async XLA Ops:
  3.6 14.5 %all-to-all-start = ((f32[8,8,512]{2,1,0:T(8,128)}), f32[8,8,512]{2,1,0:T(8,128)S(1)}, u32[]{:S(2)}, u32[]{:S(2)}) async-start(f32[8,8,512]{2,1,0:T(8,128)} %bitcast), calls=%async_computation | async-start | bytes 262144 | tf_op jit(solution)/shard_map/all_to_all | solution.py:292
  18.8 16.2 %all-to-all-start.1 = ((f32[8,8,512]{2,1,0:T(8,128)}), f32[8,8,512]{2,1,0:T(8,128)S(1)}, u32[]{:S(2)}, u32[]{:S(2)}) async-start(f32[8,8,512]{2,1,0:T(8,128)} %get-tuple-element.20), calls=%async_computation.1 | async-start | bytes 262144 | tf_op jit(solution)/shard_map/all_to_all | solution.py:295
  35.7 12.3 %all-to-all-start.2 = ((f32[8,8,512]{2,1,0:T(8,128)}), f32[8,8,512]{2,1,0:T(8,128)S(1)}, u32[]{:S(2)}, u32[]{:S(2)}) async-start(f32[8,8,512]{2,1,0:T(8,128)} %nearer.1), calls=%async_computation.2 | async-start | bytes 262144 | tf_op jit(solution)/shard_map/all_to_all | solution.py:298
  40.9 3.8 %collective-permute-start.1 = (f32[32,256]{1,0:T(8,128)S(1)}, f32[32,256]{1,0:T(8,128)S(1)}, u32[]{:S(2)}, u32[]{:S(2)}) collective-permute-start(f32[32,256]{1,0:T(8,128)S(1)} %get-tuple-element.24.refs_1_), channel_id=1, source_target_pairs={{0,2},{2,0},{1,3},{3,1},{4,6},{6,4},{5,7},{7,5},{8,10},{10,8},{9,1... | collective-permute-start | bytes 98312 | tf_op jit(solution)/shard_map/ppermute | solution.py:300
  43.9 1.2 %collective-permute-start = (f32[32,256]{1,0:T(8,128)S(1)}, f32[32,256]{1,0:T(8,128)S(1)}, u32[]{:S(2)}, u32[]{:S(2)}) collective-permute-start(f32[32,256]{1,0:T(8,128)S(1)} %get-tuple-element.23.refs_0_), channel_id=1, source_target_pairs={{0,2},{2,0},{1,3},{3,1},{4,6},{6,4},{5,7},{7,5},{8,10},{10,8},{9,1... | collective-permute-start | bytes 98312 | tf_op jit(solution)/shard_map/ppermute | solution.py:300
  50.0 6.1 %collective-permute-start.2 = (f32[3,16,512]{2,1,0:T(8,128)S(1)}, f32[3,16,512]{2,1,0:T(8,128)S(1)}, u32[]{:S(2)}, u32[]{:S(2)}) collective-permute-start(f32[3,16,512]{2,1,0:T(8,128)S(1)} %pixels_sent.1), channel_id=1, source_target_pairs={{0,2},{2,0},{1,3},{3,1},{4,6},{6,4},{5,7},{7,5},{8,10},{10,8},{9,1... | collective-permute-start | bytes 294920 | tf_op jit(solution)/shard_map/ppermute | solution.py:302

commit v4 on v0

v4 whole, which is shorter than its diff:
```python
import functools

import jax
import jax.numpy as jnp
from jax import lax
from jax.experimental import pallas as pl
from jax.experimental.pallas import tpu as pltpu
from jax.sharding import Mesh
from jax.sharding import PartitionSpec as P

LANES = 128
CHUNKS = 8
STEP = 8
WIDE = 32
LOG2E = 1.4426950408889634
VMEM = pl.BlockSpec(memory_space=pltpu.VMEM)
HBM = pl.BlockSpec(memory_space=pltpu.HBM)
PLANE = ("y", "x")


def params(mib):
    return pltpu.CompilerParams(vmem_limit_bytes=mib * 1024 * 1024)


def cost(flops, size, transcendentals=0):
    return pl.CostEstimate(flops=flops, bytes_accessed=size, transcendentals=transcendentals)


def in_hbm(*arrays):
    return [pltpu.with_memory_space_constraint(x, pltpu.HBM) for x in arrays]


def load_kernel(sizes, density_ref, ext_ref, sun_ref, sky_ref, light_ref, table_ref, held_ref, local_ref, three_ref, sems, small_sems):
    nx, ny, full_x, full_y = sizes
    tiles = held_ref.shape[0]
    planes = nx // CHUNKS
    copies = [
        [
            pltpu.make_async_copy(
                density_ref.at[pl.ds(k * planes, planes), :, pl.ds(t * LANES, LANES)],
                held_ref.at[t, pl.ds(k * planes, planes), pl.ds(0, ny)],
                sems.at[k, t],
            )
            for t in range(tiles)
        ]
        for k in range(CHUNKS)
    ]
    small = [
        pltpu.make_async_copy(source, three_ref.at[i], small_sems.at[i]) for i, source in enumerate((ext_ref, sun_ref, sky_ref))
    ]
    for chunk in copies:
        for copy in chunk:
            copy.start()
    for copy in small:
        copy.start()
    for k in range(CHUNKS):
        for t in range(tiles):
            copies[k][t].wait()
            lanes = slice(t * LANES, (t + 1) * LANES)
            for part in range(0, ny, WIDE):
                at = slice(part, part + WIDE)
                total = light_ref[at, lanes] if k else jnp.zeros((WIDE, LANES), jnp.float32)
                for x in range(k * planes, (k + 1) * planes):
                    cell = held_ref[t, x, at]
                    local_ref[t, x, at] = total + 0.5 * cell
                    total = total + cell
                light_ref[at, lanes] = total
    for copy in small:
        copy.wait()
    for c in range(3):
        row = (-LOG2E / full_y * three_ref[0, c], -LOG2E / full_x * three_ref[0, c], three_ref[1, c], three_ref[2, c])
        for i, value in enumerate(row):
            table_ref[8 * (4 * c + i) : 8 * (4 * c + i) + 8] = jnp.full((8, LANES), value, jnp.float32)


def factor(table_ref, c, which):
    return table_ref[8 * (4 * c + which) : 8 * (4 * c + which) + 8]


def load_of(density, extinction, sun_colour, sky_colour, full_x, full_y):
    nx, ny, nz = density.shape
    tiles = nz // LANES
    held = jax.ShapeDtypeStruct((tiles, nx, ny + 8, LANES), jnp.float32)
    return pl.pallas_call(
        functools.partial(load_kernel, (nx, ny, full_x, full_y)),
        in_specs=[HBM, HBM, HBM, HBM],
        out_specs=[VMEM, VMEM, VMEM, VMEM],
        out_shape=[
            jax.ShapeDtypeStruct((ny, nz), jnp.float32),
            jax.ShapeDtypeStruct((12 * 8, LANES), jnp.float32),
            held,
            held,
        ],
        scratch_shapes=[
            pltpu.SMEM((3, 3), jnp.float32),
            pltpu.SemaphoreType.DMA((CHUNKS, tiles)),
            pltpu.SemaphoreType.DMA((3,)),
        ],
        compiler_params=params(4),
        cost_estimate=cost(2**21, 2**23),
        name="load",
    )(*in_hbm(density, extinction, sun_colour, sky_colour))


def plane_kernel(own_ref, within_ref, sums_ref):
    total = jnp.zeros_like(own_ref[0])
    for k in range(own_ref.shape[0]):
        within_ref[k] = total
        total = total + own_ref[k]
    for k in range(sums_ref.shape[0]):
        sums_ref[k] = total


def plane_of(own, planes):
    _, part, nz = own.shape
    return pl.pallas_call(
        plane_kernel,
        in_specs=[VMEM],
        out_specs=[VMEM, VMEM],
        out_shape=[jax.ShapeDtypeStruct(own.shape, jnp.float32), jax.ShapeDtypeStruct((planes, part, nz), jnp.float32)],
        compiler_params=params(2),
        name="plane_sums",
    )(own)


def nearer_kernel(sums_ref, within_ref, back_ref):
    plane = lax.axis_index("z")
    total = jnp.zeros_like(sums_ref[0])
    for k in range(sums_ref.shape[0] - 1):
        total = total + sums_ref[k] * (k < plane).astype(jnp.float32)
    for k in range(within_ref.shape[0]):
        back_ref[k] = within_ref[k] + total


def nearer_of(sums, within):
    return pl.pallas_call(
        nearer_kernel,
        in_specs=[VMEM, VMEM],
        out_specs=VMEM,
        out_shape=jax.ShapeDtypeStruct(within.shape, jnp.float32),
        compiler_params=params(2),
        name="nearer",
    )(sums, within)


def pixel_kernel(own, sizes, table_ref, before_ref, held_ref, local_ref, out_ref, a_ref):
    nx, ny = sizes
    pitch = ny + 8
    tiles, _, _ = held_ref.shape
    rows = nx // 2
    for c in range(3):
        rate, colour = factor(table_ref, c, 1)[:1], factor(table_ref, c, 2)[:1]
        for t in range(tiles):
            a_ref[c, t] = colour * jnp.exp2(before_ref[:, t * LANES : (t + 1) * LANES] * rate)
    half = lax.axis_index("depth")
    start = (half if own else 1 - half) * rows
    view_rate = [factor(table_ref, c, 0) for c in range(3)]
    sun_rate = [factor(table_ref, c, 1) for c in range(3)]
    zero, one = jnp.zeros((8, LANES), jnp.float32), jnp.ones((8, LANES), jnp.float32)
    for tile in range(tiles):

        def cells(step, state, tile=tile):
            view = list(state[0])
            passing, total = ([list(p) for p in q] for q in state[1:])
            for k in range(STEP):
                y = step * STEP + k
                light = [jnp.broadcast_to(a_ref[c, tile, pl.ds(y, 1), :], (8, LANES)) for c in range(3)]
                for t in range(2):
                    at = pl.ds((start + 8 * t) * pitch + y, 8, stride=pitch)
                    view[t] = view[t] + held_ref[tile, at, :]
                    sun = local_ref[tile, at, :]
                    for c in range(3):
                        later = jnp.exp2(view[t] * view_rate[c])
                        total[c][t] = total[c][t] + (passing[c][t] - later) * (jnp.exp2(sun * sun_rate[c]) * light[c])
                        passing[c][t] = later
            return tuple(view), *(tuple(tuple(p) for p in q) for q in (passing, total))

        view, _, total = lax.fori_loop(0, ny // STEP, cells, ((zero, zero), ((one, one),) * 3, ((zero, zero),) * 3))
        lanes = slice(tile * LANES, (tile + 1) * LANES)
        for t in range(2):
            for c in range(3):
                out_ref[c, 8 * t : 8 * t + 8, lanes] = total[c][t]
            out_ref[3, 8 * t : 8 * t + 8, lanes] = view[t]


def pixels_of(own, before, table, held, local, name):
    ny, nz = before.shape
    tiles, nx, pitch, _ = held.shape
    flat = (tiles, nx * pitch, LANES)
    return pl.pallas_call(
        functools.partial(pixel_kernel, own, (nx, ny)),
        in_specs=[VMEM] * 4,
        out_specs=VMEM,
        out_shape=jax.ShapeDtypeStruct((4, nx // 2, nz), jnp.float32),
        scratch_shapes=[pltpu.VMEM((3, tiles, ny, LANES), jnp.float32)],
        compiler_params=params(4),
        cost_estimate=cost(2**24, 2**22, 2**21),
        name=name,
    )(table, before, held.reshape(flat), local.reshape(flat))


def image_kernel(table_ref, kept_ref, received_ref, image_ref, passed_ref):
    _, rows, nz = image_ref.shape
    near = lax.axis_index("depth") == 0
    for row in range(0, rows, 8):
        for lane in range(0, nz, LANES):
            at = (slice(row, row + 8), slice(lane, lane + LANES))
            mine, other = kept_ref[(3, *at)], received_ref[(3, *at)]
            front = jnp.where(near, mine, other)
            behind = jnp.where(near, other, mine)
            for c in range(3):
                rate = factor(table_ref, c, 0)
                passing = jnp.exp2(front * rate)
                passed = jnp.exp2((front + behind) * rate)
                mine_c, other_c = kept_ref[(c, *at)], received_ref[(c, *at)]
                near_c, far_c = jnp.where(near, mine_c, other_c), jnp.where(near, other_c, mine_c)
                passed_ref[(c, *at)] = passed
                image_ref[(c, *at)] = near_c + passing * far_c + factor(table_ref, c, 3) * passed


def image_of(table, kept, received):
    _, rows, nz = kept.shape
    shape = jax.ShapeDtypeStruct((3, rows, nz), jnp.float32)
    return pl.pallas_call(
        image_kernel,
        in_specs=[VMEM] * 3,
        out_specs=[VMEM, VMEM],
        out_shape=[shape, shape],
        compiler_params=params(4),
        name="image",
    )(table, kept, received)


def per_device(sizes, density, extinction, sun_colour, sky_colour):
    planes, members, full_x, full_y = sizes
    _, ny, nz = density.shape
    deal = functools.partial(lax.all_to_all, split_axis=0, concat_axis=0, tiled=True)
    column_light, table, held, local = load_of(density, extinction, sun_colour, sky_colour, full_x, full_y)
    within, sums = plane_of(deal(column_light.reshape(members, ny // members, nz), PLANE), planes)
    before = deal(nearer_of(deal(sums, "z"), within), PLANE).reshape(ny, nz)
    sent = pixels_of(False, before, table, held, local, "pixels_sent")
    received = lax.ppermute(sent, "depth", [(0, 1), (1, 0)])
    kept = pixels_of(True, before, table, held, local, "pixels_kept")
    return image_of(table, kept, received)


def solution(mesh):
    shape = (8, 4, 2, 2, 2)
    fine = Mesh(mesh.devices.reshape(shape), ("z", *PLANE, "depth", "tile"))
    light = ("z", *PLANE)
    sizes = (8, 8, 2048, 128)
    return jax.shard_map(
        functools.partial(per_device, sizes),
        mesh=fine,
        in_specs=(P(light, "depth", "tile"), P(), P(), P()),
        out_specs=(P(None, (*light, "depth"), "tile"), P(None, (*light, "depth"), "tile")),
        check_vma=False,
    )
```

time: 269 us -> 53.3 us (0.20)
  waiting for transfers between devices: 153 us -> 0.01 us
  other arithmetic: 89.2 us -> 0 us
  blocking collectives: 4.96 us -> 39.8 us
  between operations: 17.4 us -> 0.67 us
  Pallas kernels: 0 us -> 7.93 us
  starting transfers between devices: 0.12 us -> 4.7 us
    all_gather x1 -> x0, waiting for transfers between devices: 139 us -> none  [prefix(): everything = lax.all_gather(value, axis)]
    select_n x66 -> x0, other arithmetic: 61.4 us -> none  [hop(): return jnp.where(reached, new, before)]
    all_to_all x0 -> x3, blocking collectives: none -> 39.8 us  [the longest x2 25.5 us: per_device(): before = deal(nearer_of(deal(sums, 'z'), within), PLANE).reshape(ny, nz)]
    another operation x3 -> x0, other arithmetic: 22.5 us -> none  [the longest x1 17.3 us: per_device(): local_view = (jnp.cumsum(density, axis=1) - density) / full_y]
    reduce_scatter x2 -> x0, waiting for transfers between devices: 13 us -> none  [the longest x1 12.9 us: per_device(): lax.psum_scatter(contribution, 'depth', scatter_dimension=1, tiled=True)]
    pallas_call x0 -> x6, Pallas kernels: none -> 7.93 us  [the longest x2 4.48 us: pixels_of(): pl.pallas_call(functools.partial(pixel_kernel, own, (nx, ny)), in_specs=[...]
    all_gather x1 -> x0, blocking collectives: 4.96 us -> none  [prefix(): everything = lax.all_gather(value, axis)]
    ppermute x0 -> x1, starting transfers between devices: none -> 4.7 us  [per_device(): received = lax.ppermute(sent, 'depth', [(0, 1), (1, 0)])]
  transfers between devices with their start and end apart: 3 -> 1, of which waited for: 2 -> 0; matrix products, arithmetic and copies ran while one was open for 32% -> 0% of each run, Pallas kernels for 0% -> 4%
where the time goes in v4:
time: 53.3 us; the launch traced here: 53.1 us
  blocking collectives  39.8 us (75%)
  Pallas kernels  7.93 us (15%)
  starting transfers between devices  4.7 us (9%)
  between operations  0.67 us (1%)
    all_to_all x2, blocking collectives, per_device(): before = deal(nearer_of(deal(sums, 'z'), within), PLANE).reshape(ny, nz)  25.5 us
    all_to_all x1, blocking collectives, per_device(): deal(column_light.reshape(members, ny // members, nz), PLANE)  14.3 us
    ppermute x1, starting transfers between devices, per_device(): received = lax.ppermute(sent, 'depth', [(0, 1), (1, 0)])  4.7 us
    pallas_call x2, Pallas kernels, pixels_of(): pl.pallas_call(functools.partial(pixel_kernel, own, (nx, ny)), in_specs=[...  4.48 us
    pallas_call x1, Pallas kernels, load_of(): pl.pallas_call(functools.partial(load_kernel, (nx, ny, full_x, full_y)),...  2.68 us
  transfers between devices with their start and end apart: 1, of which 0 were waited for; matrix products, arithmetic and copies ran while one was open for 0% of the time, Pallas kernels for 4%

profile of v4, /device:TPU:1, one launch (start us, length us, event | category | flops | bytes accessed | tf_op | source)
XLA Modules:
  0.0 53.1 jit_solution(17468617352414822396)
XLA Ops:
  0.6 2.7 %load.1 = (f32[64,512]{1,0:T(8,128)S(1)}, f32[96,128]{1,0:T(8,128)S(1)}, f32[4,32,72,128]{3,2,1,0:T(8,128)S(1)}, f32[4,32,72,128]{3,2,1,0:T(8,128)S(1)}) custom-call(f32[32,64,512]{2,1,0:T(8,128)} %density_ref.1, f32[3]{0:T(128)} %ext_ref.1, f32[3]{0:T(128)} %sun_ref.1, f32[3]{0:T(128)} %sky_ref.1), custom_call_target="tpu_custom_call" | custom-call | flops 2097152 | bytes 8388608 | tf_op jit(solution)/shard_map/load/pallas_call | solution.py:84
  3.3 14.3 %all_to_all.15.own_ref = f32[8,8,512]{2,1,0:T(8,128)S(1)} all-to-all(f32[8,8,512]{2,1,0:T(8,128)S(1)} %bitcast.10), channel_id=1, replica_groups=mesh['z'=8,'y'=4,'x'=2,'depth'=2,'tile'=2] {'y','x'}, dimensions={0} | all-to-all | bytes 262144 | tf_op jit(solution)/shard_map/all_to_all | solution.py:239
  17.7 16.0 %all_to_all.16.sums_ref = f32[8,8,512]{2,1,0:T(8,128)S(1)} all-to-all(f32[8,8,512]{2,1,0:T(8,128)S(1)} %get-tuple-element.10), channel_id=1, replica_groups=mesh['z'=8,'y'=4,'x'=2,'depth'=2,'tile'=2] {'z'}, dimensions={0} | all-to-all | bytes 262144 | tf_op jit(solution)/shard_map/all_to_all | solution.py:240
  33.7 9.4 %all_to_all.17 = f32[8,8,512]{2,1,0:T(8,128)S(1)} all-to-all(f32[8,8,512]{2,1,0:T(8,128)S(1)} %nearer.1), channel_id=1, replica_groups=mesh['z'=8,'y'=4,'x'=2,'depth'=2,'tile'=2] {'y','x'}, dimensions={0} | all-to-all | bytes 262144 | tf_op jit(solution)/shard_map/all_to_all | solution.py:240
  43.1 2.2 %pixels_sent.1 = f32[4,16,512]{2,1,0:T(8,128)S(1)} custom-call(f32[96,128]{1,0:T(8,128)S(1)} %get-tuple-element.8.table_ref, f32[64,512]{1,0:T(8,128)S(1)} %bitcast.8, f32[4,2304,128]{2,1,0:T(8,128)S(1)} %bitcast.4, f32[4,2304,128]{2,1,0:T(8,128)S(1)} %bitcast.6), custom_call_target="tpu_custom_call" | custom-call | flops 16777216 | bytes 4194304 | tf_op jit(solution)/shard_map/pixels_sent/pallas_call | solution.py:190
  45.4 4.7 %collective-permute-start = (f32[4,16,512]{2,1,0:T(8,128)S(1)}, f32[4,16,512]{2,1,0:T(8,128)S(1)}, u32[]{:S(2)}, u32[]{:S(2)}) collective-permute-start(f32[4,16,512]{2,1,0:T(8,128)S(1)} %pixels_sent.1), channel_id=1, source_target_pairs={{0,2},{2,0},{1,3},{3,1},{4,6},{6,4},{5,7},{7,5},{8,10},{10,8},{9,1... | collective-permute-start | bytes 393224 | tf_op jit(solution)/shard_map/ppermute | solution.py:242
  50.1 2.2 %pixels_kept.1.kept_ref = f32[4,16,512]{2,1,0:T(8,128)S(1)} custom-call(f32[96,128]{1,0:T(8,128)S(1)} %get-tuple-element.8.table_ref, f32[64,512]{1,0:T(8,128)S(1)} %bitcast.9, f32[4,2304,128]{2,1,0:T(8,128)S(1)} %bitcast.5, f32[4,2304,128]{2,1,0:T(8,128)S(1)} %bitcast.7), custom_call_target="tpu_custom_call" | custom-call | flops 16777216 | bytes 4194304 | tf_op jit(solution)/shard_map/pixels_kept/pallas_call | solution.py:190
  52.4 0.0 collective-permute-done.received_ref
  52.4 0.7 %image.1 = (f32[3,16,512]{2,1,0:T(8,128)}, f32[3,16,512]{2,1,0:T(8,128)}) custom-call(f32[96,128]{1,0:T(8,128)S(1)} %get-tuple-element.8.table_ref, f32[4,16,512]{2,1,0:T(8,128)S(1)} %pixels_kept.1.kept_ref, f32[4,16,512]{2,1,0:T(8,128)S(1)} %collective-permute-done.received_ref), custom_call_target="tpu_custom_call" | custom-call | tf_op jit(solution)/shard_map/image/pallas_call | solution.py:224
  (2 shorter events, 0.0 us)
Async XLA Ops:
  45.4 7.0 %collective-permute-start = (f32[4,16,512]{2,1,0:T(8,128)S(1)}, f32[4,16,512]{2,1,0:T(8,128)S(1)}, u32[]{:S(2)}, u32[]{:S(2)}) collective-permute-start(f32[4,16,512]{2,1,0:T(8,128)S(1)} %pixels_sent.1), channel_id=1, source_target_pairs={{0,2},{2,0},{1,3},{3,1},{4,6},{6,4},{5,7},{7,5},{8,10},{10,8},{9,1... | collective-permute-start | bytes 393224 | tf_op jit(solution)/shard_map/ppermute | solution.py:242

commit v5 on v4

--- a/solution.py
+++ b/solution.py
@@ -15,7 +15,6 @@
 LOG2E = 1.4426950408889634
 VMEM = pl.BlockSpec(memory_space=pltpu.VMEM)
 HBM = pl.BlockSpec(memory_space=pltpu.HBM)
-PLANE = ("y", "x")
 
 
 def params(mib):
@@ -30,7 +29,7 @@
     return [pltpu.with_memory_space_constraint(x, pltpu.HBM) for x in arrays]
 
 
-def load_kernel(sizes, density_ref, ext_ref, sun_ref, sky_ref, light_ref, table_ref, held_ref, local_ref, three_ref, sems, small_sems):
+def load_kernel(sizes, density_ref, ext_ref, sun_ref, sky_ref, light_ref, table_ref, held_ref, local_ref, sums_ref, three_ref, sems, small_sems):
     nx, ny, full_x, full_y = sizes
     tiles = held_ref.shape[0]
     planes = nx // CHUNKS
@@ -56,15 +55,16 @@
     for k in range(CHUNKS):
         for t in range(tiles):
             copies[k][t].wait()
-            lanes = slice(t * LANES, (t + 1) * LANES)
             for part in range(0, ny, WIDE):
                 at = slice(part, part + WIDE)
-                total = light_ref[at, lanes] if k else jnp.zeros((WIDE, LANES), jnp.float32)
+                total = sums_ref[t, at] if k else jnp.zeros((WIDE, LANES), jnp.float32)
                 for x in range(k * planes, (k + 1) * planes):
                     cell = held_ref[t, x, at]
                     local_ref[t, x, at] = total + 0.5 * cell
                     total = total + cell
-                light_ref[at, lanes] = total
+                sums_ref[t, at] = total
+    for t in range(tiles):
+        light_ref[pl.ds(t, ny, stride=tiles), :] = sums_ref[t]
     for copy in small:
         copy.wait()
     for c in range(3):
@@ -86,12 +86,13 @@
         in_specs=[HBM, HBM, HBM, HBM],
         out_specs=[VMEM, VMEM, VMEM, VMEM],
         out_shape=[
-            jax.ShapeDtypeStruct((ny, nz), jnp.float32),
+            jax.ShapeDtypeStruct((ny * tiles, LANES), jnp.float32),
             jax.ShapeDtypeStruct((12 * 8, LANES), jnp.float32),
             held,
             held,
         ],
         scratch_shapes=[
+            pltpu.VMEM((tiles, ny, LANES), jnp.float32),
             pltpu.SMEM((3, 3), jnp.float32),
             pltpu.SemaphoreType.DMA((CHUNKS, tiles)),
             pltpu.SemaphoreType.DMA((3,)),
@@ -102,45 +103,26 @@
     )(*in_hbm(density, extinction, sun_colour, sky_colour))
 
 
-def plane_kernel(own_ref, within_ref, sums_ref):
+def before_kernel(own_ref, dealt_ref):
+    near = (lax.axis_index("x") == 0).astype(jnp.float32)
     total = jnp.zeros_like(own_ref[0])
     for k in range(own_ref.shape[0]):
-        within_ref[k] = total
-        total = total + own_ref[k]
-    for k in range(sums_ref.shape[0]):
-        sums_ref[k] = total
-
-
-def plane_of(own, planes):
-    _, part, nz = own.shape
-    return pl.pallas_call(
-        plane_kernel,
+        own = own_ref[k]
+        dealt_ref[2 * k] = total
+        dealt_ref[2 * k + 1] = total + near * own
+        total = total + own
+
+
+def before_of(own):
+    pairs, rows, lanes = own.shape
+    return pl.pallas_call(
+        before_kernel,
         in_specs=[VMEM],
-        out_specs=[VMEM, VMEM],
-        out_shape=[jax.ShapeDtypeStruct(own.shape, jnp.float32), jax.ShapeDtypeStruct((planes, part, nz), jnp.float32)],
+        out_specs=VMEM,
+        out_shape=jax.ShapeDtypeStruct((2 * pairs, rows, lanes), jnp.float32),
         compiler_params=params(2),
-        name="plane_sums",
+        name="before",
     )(own)
-
-
-def nearer_kernel(sums_ref, within_ref, back_ref):
-    plane = lax.axis_index("z")
-    total = jnp.zeros_like(sums_ref[0])
-    for k in range(sums_ref.shape[0] - 1):
-        total = total + sums_ref[k] * (k < plane).astype(jnp.float32)
-    for k in range(within_ref.shape[0]):
-        back_ref[k] = within_ref[k] + total
-
-
-def nearer_of(sums, within):
-    return pl.pallas_call(
-        nearer_kernel,
-        in_specs=[VMEM, VMEM],
-        out_specs=VMEM,
-        out_shape=jax.ShapeDtypeStruct(within.shape, jnp.float32),
-        compiler_params=params(2),
-        name="nearer",
-    )(sums, within)
 
 
 def pixel_kernel(own, sizes, table_ref, before_ref, held_ref, local_ref, out_ref, a_ref):
@@ -149,9 +131,9 @@
     tiles, _, _ = held_ref.shape
     rows = nx // 2
     for c in range(3):
-        rate, colour = factor(table_ref, c, 1)[:1], factor(table_ref, c, 2)[:1]
-        for t in range(tiles):
-            a_ref[c, t] = colour * jnp.exp2(before_ref[:, t * LANES : (t + 1) * LANES] * rate)
+        rate, colour = factor(table_ref, c, 1), factor(table_ref, c, 2)
+        for k in range(before_ref.shape[0] // 2):
+            a_ref[c, 8 * k : 8 * k + 8] = colour * jnp.exp2((before_ref[2 * k] + before_ref[2 * k + 1]) * rate)
     half = lax.axis_index("depth")
     start = (half if own else 1 - half) * rows
     view_rate = [factor(table_ref, c, 0) for c in range(3)]
@@ -164,7 +146,7 @@
             passing, total = ([list(p) for p in q] for q in state[1:])
             for k in range(STEP):
                 y = step * STEP + k
-                light = [jnp.broadcast_to(a_ref[c, tile, pl.ds(y, 1), :], (8, LANES)) for c in range(3)]
+                light = [jnp.broadcast_to(a_ref[c, pl.ds(y * tiles + tile, 1), :], (8, LANES)) for c in range(3)]
                 for t in range(2):
                     at = pl.ds((start + 8 * t) * pitch + y, 8, stride=pitch)
                     view[t] = view[t] + held_ref[tile, at, :]
@@ -184,15 +166,15 @@
 
 
 def pixels_of(own, before, table, held, local, name):
-    ny, nz = before.shape
     tiles, nx, pitch, _ = held.shape
+    ny, nz = pitch - 8, tiles * LANES
     flat = (tiles, nx * pitch, LANES)
     return pl.pallas_call(
         functools.partial(pixel_kernel, own, (nx, ny)),
         in_specs=[VMEM] * 4,
         out_specs=VMEM,
         out_shape=jax.ShapeDtypeStruct((4, nx // 2, nz), jnp.float32),
-        scratch_shapes=[pltpu.VMEM((3, tiles, ny, LANES), jnp.float32)],
+        scratch_shapes=[pltpu.VMEM((3, ny * tiles, LANES), jnp.float32)],
         compiler_params=params(4),
         cost_estimate=cost(2**24, 2**22, 2**21),
         name=name,
@@ -232,12 +214,11 @@
 
 
 def per_device(sizes, density, extinction, sun_colour, sky_colour):
-    planes, members, full_x, full_y = sizes
-    _, ny, nz = density.shape
+    pairs, full_x, full_y = sizes
     deal = functools.partial(lax.all_to_all, split_axis=0, concat_axis=0, tiled=True)
     column_light, table, held, local = load_of(density, extinction, sun_colour, sky_colour, full_x, full_y)
-    within, sums = plane_of(deal(column_light.reshape(members, ny // members, nz), PLANE), planes)
-    before = deal(nearer_of(deal(sums, "z"), within), PLANE).reshape(ny, nz)
+    own = deal(column_light.reshape(pairs, -1, LANES), ("z", "y"))
+    before = deal(before_of(own), ("z", "y", "x"))
     sent = pixels_of(False, before, table, held, local, "pixels_sent")
     received = lax.ppermute(sent, "depth", [(0, 1), (1, 0)])
     kept = pixels_of(True, before, table, held, local, "pixels_kept")
@@ -246,9 +227,9 @@
 
 def solution(mesh):
     shape = (8, 4, 2, 2, 2)
-    fine = Mesh(mesh.devices.reshape(shape), ("z", *PLANE, "depth", "tile"))
-    light = ("z", *PLANE)
-    sizes = (8, 8, 2048, 128)
+    light = ("z", "y", "x")
+    fine = Mesh(mesh.devices.reshape(shape), (*light, "depth", "tile"))
+    sizes = (32, 2048, 128)
     return jax.shard_map(
         functools.partial(per_device, sizes),
         mesh=fine,

time: 53.3 us -> 52.3 us (0.981)
  starting transfers between devices: 4.7 us -> 3.82 us
    ppermute x1, starting transfers between devices: 4.7 us -> 3.82 us  [per_device(): received = lax.ppermute(sent, 'depth', [(0, 1), (1, 0)])]
    all_to_all x3 -> x2, blocking collectives: 39.8 us -> 39.7 us  [the longest x1 21.2 us: per_device(): own = deal(column_light.reshape(pairs, -1, LANES), ('z', 'y'))]
where the time goes in v5:
time: 52.3 us; the launch traced here: 52.1 us
  blocking collectives  39.7 us (76%)
  Pallas kernels  7.94 us (15%)
  starting transfers between devices  3.82 us (7%)
  between operations  0.66 us (1%)
    all_to_all x1, blocking collectives, per_device(): own = deal(column_light.reshape(pairs, -1, LANES), ('z', 'y'))  21.2 us
    all_to_all x1, blocking collectives, per_device(): before = deal(before_of(own), ('z', 'y', 'x'))  18.5 us
    pallas_call x2, Pallas kernels, pixels_of(): pl.pallas_call(functools.partial(pixel_kernel, own, (nx, ny)), in_specs=[...  4.49 us
    ppermute x1, starting transfers between devices, per_device(): received = lax.ppermute(sent, 'depth', [(0, 1), (1, 0)])  3.82 us
    pallas_call x1, Pallas kernels, load_of(): pl.pallas_call(functools.partial(load_kernel, (nx, ny, full_x, full_y)),...  2.68 us
  transfers between devices with their start and end apart: 1, of which 0 were waited for; matrix products, arithmetic and copies ran while one was open for 0% of the time, Pallas kernels for 4%

profile of v5, /device:TPU:1, one launch (start us, length us, event | category | flops | bytes accessed | tf_op | source)
XLA Modules:
  0.0 52.1 jit_solution(5011947853587410532)
XLA Ops:
  0.6 2.7 %load.1 = (f32[256,128]{1,0:T(8,128)S(1)}, f32[96,128]{1,0:T(8,128)S(1)}, f32[4,32,72,128]{3,2,1,0:T(8,128)S(1)}, f32[4,32,72,128]{3,2,1,0:T(8,128)S(1)}) custom-call(f32[32,64,512]{2,1,0:T(8,128)} %density_ref.1, f32[3]{0:T(128)} %ext_ref.1, f32[3]{0:T(128)} %sun_ref.1, f32[3]{0:T(128)} %sky_ref.1), custom_call_target="tpu_custom_call" | custom-call | flops 2097152 | bytes 8388608 | tf_op jit(solution)/shard_map/load/pallas_call | solution.py:84
  3.3 21.2 %all_to_all.10.own_ref = f32[32,8,128]{2,1,0:T(8,128)S(1)} all-to-all(f32[32,8,128]{2,1,0:T(8,128)S(1)} %bitcast.7), channel_id=1, replica_groups=mesh['z'=8,'y'=4,'x'=2,'depth'=2,'tile'=2] {'z','y'}, dimensions={0} | all-to-all | bytes 262144 | tf_op jit(solution)/shard_map/all_to_all | solution.py:220
  24.5 18.5 %all_to_all.11.before_ref = f32[64,8,128]{2,1,0:T(8,128)S(1)} all-to-all(f32[64,8,128]{2,1,0:T(8,128)S(1)} %before.1), channel_id=1, replica_groups=mesh['z'=8,'y'=4,'x'=2,'depth'=2,'tile'=2] {'z','y','x'}, dimensions={0} | all-to-all | bytes 524288 | tf_op jit(solution)/shard_map/all_to_all | solution.py:221
  43.0 2.2 %pixels_sent.1 = f32[4,16,512]{2,1,0:T(8,128)S(1)} custom-call(f32[96,128]{1,0:T(8,128)S(1)} %get-tuple-element.6.table_ref, f32[64,8,128]{2,1,0:T(8,128)S(1)} %all_to_all.11.before_ref, f32[4,2304,128]{2,1,0:T(8,128)S(1)} %bitcast.3, f32[4,2304,128]{2,1,0:T(8,128)S(1)} %bitcast.5), custom_call_target="tpu_custom_call" | custom-call | flops 16777216 | bytes 4194304 | tf_op jit(solution)/shard_map/pixels_sent/pallas_call | solution.py:172
  45.3 3.8 %collective-permute-start = (f32[4,16,512]{2,1,0:T(8,128)S(1)}, f32[4,16,512]{2,1,0:T(8,128)S(1)}, u32[]{:S(2)}, u32[]{:S(2)}) collective-permute-start(f32[4,16,512]{2,1,0:T(8,128)S(1)} %pixels_sent.1), channel_id=1, source_target_pairs={{0,2},{2,0},{1,3},{3,1},{4,6},{6,4},{5,7},{7,5},{8,10},{10,8},{9,1... | collective-permute-start | bytes 393224 | tf_op jit(solution)/shard_map/ppermute | solution.py:223
  49.1 2.2 %pixels_kept.1.kept_ref = f32[4,16,512]{2,1,0:T(8,128)S(1)} custom-call(f32[96,128]{1,0:T(8,128)S(1)} %get-tuple-element.6.table_ref, f32[64,8,128]{2,1,0:T(8,128)S(1)} %all_to_all.11.before_ref, f32[4,2304,128]{2,1,0:T(8,128)S(1)} %bitcast.4, f32[4,2304,128]{2,1,0:T(8,128)S(1)} %bitcast.6), custom_call_target="tpu_custom_call" | custom-call | flops 16777216 | bytes 4194304 | tf_op jit(solution)/shard_map/pixels_kept/pallas_call | solution.py:172
  51.4 0.0 collective-permute-done.received_ref
  51.4 0.7 %image.1 = (f32[3,16,512]{2,1,0:T(8,128)}, f32[3,16,512]{2,1,0:T(8,128)}) custom-call(f32[96,128]{1,0:T(8,128)S(1)} %get-tuple-element.6.table_ref, f32[4,16,512]{2,1,0:T(8,128)S(1)} %pixels_kept.1.kept_ref, f32[4,16,512]{2,1,0:T(8,128)S(1)} %collective-permute-done.received_ref), custom_call_target="tpu_custom_call" | custom-call | tf_op jit(solution)/shard_map/image/pallas_call | solution.py:206
  (1 shorter events, 0.0 us)
Async XLA Ops:
  45.3 6.1 %collective-permute-start = (f32[4,16,512]{2,1,0:T(8,128)S(1)}, f32[4,16,512]{2,1,0:T(8,128)S(1)}, u32[]{:S(2)}, u32[]{:S(2)}) collective-permute-start(f32[4,16,512]{2,1,0:T(8,128)S(1)} %pixels_sent.1), channel_id=1, source_target_pairs={{0,2},{2,0},{1,3},{3,1},{4,6},{6,4},{5,7},{7,5},{8,10},{10,8},{9,1... | collective-permute-start | bytes 393224 | tf_op jit(solution)/shard_map/ppermute | solution.py:223

commit v6 on v5

--- a/solution.py
+++ b/solution.py
@@ -11,6 +11,8 @@
 LANES = 128
 CHUNKS = 8
 STEP = 8
+PITCH = 72
+AHEAD = 3
 WIDE = 32
 LOG2E = 1.4426950408889634
 VMEM = pl.BlockSpec(memory_space=pltpu.VMEM)
@@ -29,7 +31,7 @@
     return [pltpu.with_memory_space_constraint(x, pltpu.HBM) for x in arrays]
 
 
-def load_kernel(sizes, density_ref, ext_ref, sun_ref, sky_ref, light_ref, table_ref, held_ref, local_ref, sums_ref, three_ref, sems, small_sems):
+def load_kernel(sizes, density_ref, ext_ref, sun_ref, sky_ref, light_ref, table_ref, held_ref, local_ref, view_ref, ready_ref, sums_ref, three_ref, sems, small_sems):
     nx, ny, full_x, full_y = sizes
     tiles = held_ref.shape[0]
     planes = nx // CHUNKS
@@ -72,6 +74,47 @@
         for i, value in enumerate(row):
             table_ref[8 * (4 * c + i) : 8 * (4 * c + i) + 8] = jnp.full((8, LANES), value, jnp.float32)
 
+    @pl.when(lax.axis_index("z") < AHEAD)
+    def _():
+        flat = (nx * PITCH, LANES)
+        for t in range(tiles):
+            held, local = held_ref.at[t].reshape(*flat), local_ref.at[t].reshape(*flat)
+            for start in range(0, nx, 16):
+
+                def keep(y, i, c, light, t=t, start=start):
+                    ready_ref[t, c, pl.ds((start + 8 * i) * PITCH + y, 8, stride=PITCH), :] = light
+
+                view, _ = march(table_ref, held, local, start, ny, keep)
+                for i in range(2):
+                    view_ref[start + 8 * i : start + 8 * i + 8, t * LANES : (t + 1) * LANES] = view[i]
+
+
+def march(table_ref, held_ref, local_ref, start, ny, use, state=()):
+    view_rate = [factor(table_ref, c, 0) for c in range(3)]
+    sun_rate = [factor(table_ref, c, 1) for c in range(3)]
+    zero, one = jnp.zeros((8, LANES), jnp.float32), jnp.ones((8, LANES), jnp.float32)
+
+    def cells(step, carry):
+        view, passing, state = list(carry[0]), [list(p) for p in carry[1]], carry[2]
+        for k in range(STEP):
+            y = step * STEP + k
+            for i in range(2):
+                at = pl.ds((start + 8 * i) * PITCH + y, 8, stride=PITCH)
+                view[i] = view[i] + held_ref[at, :]
+                sun = local_ref[at, :]
+                for c in range(3):
+                    later = jnp.exp2(view[i] * view_rate[c])
+                    light = (passing[c][i] - later) * jnp.exp2(sun * sun_rate[c])
+                    passing[c][i] = later
+                    if state:
+                        state = use(y, i, c, light, state)
+                    else:
+                        use(y, i, c, light)
+        return tuple(view), tuple(tuple(p) for p in passing), state
+
+    view, _, state = lax.fori_loop(0, ny // STEP, cells, ((zero, zero), ((one, one),) * 3, state))
+    return view, state
+
 
 def factor(table_ref, c, which):
     return table_ref[8 * (4 * c + which) : 8 * (4 * c + which) + 8]
@@ -80,16 +123,18 @@
 def load_of(density, extinction, sun_colour, sky_colour, full_x, full_y):
     nx, ny, nz = density.shape
     tiles = nz // LANES
-    held = jax.ShapeDtypeStruct((tiles, nx, ny + 8, LANES), jnp.float32)
+    held = jax.ShapeDtypeStruct((tiles, nx, PITCH, LANES), jnp.float32)
     return pl.pallas_call(
         functools.partial(load_kernel, (nx, ny, full_x, full_y)),
         in_specs=[HBM, HBM, HBM, HBM],
-        out_specs=[VMEM, VMEM, VMEM, VMEM],
+        out_specs=[VMEM] * 6,
         out_shape=[
             jax.ShapeDtypeStruct((ny * tiles, LANES), jnp.float32),
             jax.ShapeDtypeStruct((12 * 8, LANES), jnp.float32),
             held,
             held,
+            jax.ShapeDtypeStruct((nx, nz), jnp.float32),
+            jax.ShapeDtypeStruct((tiles, 3, nx * PITCH, LANES), jnp.float32),
         ],
         scratch_shapes=[
             pltpu.VMEM((tiles, ny, LANES), jnp.float32),
@@ -125,9 +170,8 @@
     )(own)
 
 
-def pixel_kernel(own, sizes, table_ref, before_ref, held_ref, local_ref, out_ref, a_ref):
+def pixel_kernel(own, sizes, table_ref, before_ref, held_ref, local_ref, view_ref, ready_ref, out_ref, a_ref):
     nx, ny = sizes
-    pitch = ny + 8
     tiles, _, _ = held_ref.shape
     rows = nx // 2
     for c in range(3):
@@ -136,49 +180,54 @@
             a_ref[c, 8 * k : 8 * k + 8] = colour * jnp.exp2((before_ref[2 * k] + before_ref[2 * k + 1]) * rate)
     half = lax.axis_index("depth")
     start = (half if own else 1 - half) * rows
-    view_rate = [factor(table_ref, c, 0) for c in range(3)]
-    sun_rate = [factor(table_ref, c, 1) for c in range(3)]
-    zero, one = jnp.zeros((8, LANES), jnp.float32), jnp.ones((8, LANES), jnp.float32)
-    for tile in range(tiles):
-
-        def cells(step, state, tile=tile):
-            view = list(state[0])
-            passing, total = ([list(p) for p in q] for q in state[1:])
-            for k in range(STEP):
-                y = step * STEP + k
-                light = [jnp.broadcast_to(a_ref[c, pl.ds(y * tiles + tile, 1), :], (8, LANES)) for c in range(3)]
-                for t in range(2):
-                    at = pl.ds((start + 8 * t) * pitch + y, 8, stride=pitch)
-                    view[t] = view[t] + held_ref[tile, at, :]
-                    sun = local_ref[tile, at, :]
-                    for c in range(3):
-                        later = jnp.exp2(view[t] * view_rate[c])
-                        total[c][t] = total[c][t] + (passing[c][t] - later) * (jnp.exp2(sun * sun_rate[c]) * light[c])
-                        passing[c][t] = later
-            return tuple(view), *(tuple(tuple(p) for p in q) for q in (passing, total))
-
-        view, _, total = lax.fori_loop(0, ny // STEP, cells, ((zero, zero), ((one, one),) * 3, ((zero, zero),) * 3))
-        lanes = slice(tile * LANES, (tile + 1) * LANES)
-        for t in range(2):
+    ahead = lax.axis_index("z") < AHEAD
+
+    @pl.when(ahead)
+    def _():
+        out_ref[3] = view_ref[pl.ds(pl.multiple_of(start, 8), rows), :]
+        for t in range(tiles):
             for c in range(3):
-                out_ref[c, 8 * t : 8 * t + 8, lanes] = total[c][t]
-            out_ref[3, 8 * t : 8 * t + 8, lanes] = view[t]
-
-
-def pixels_of(own, before, table, held, local, name):
-    tiles, nx, pitch, _ = held.shape
-    ny, nz = pitch - 8, tiles * LANES
-    flat = (tiles, nx * pitch, LANES)
+                light = a_ref[c, pl.ds(t, ny, stride=tiles), :].reshape(ny // 8, 8, LANES)
+                for row in range(0, rows, 8):
+                    parts = []
+                    for x in range(8):
+                        at = pl.ds(pl.multiple_of((start + row + x) * PITCH, 8), ny)
+                        cells = ready_ref[t, c, at, :].reshape(ny // 8, 8, LANES)
+                        parts.append(jnp.sum(light * cells, axis=0))
+                    out_ref[c, row : row + 8, t * LANES : (t + 1) * LANES] = jnp.sum(jnp.stack(parts), axis=1)
+
+    @pl.when(jnp.logical_not(ahead))
+    def _():
+        for t in range(tiles):
+
+            def add(y, i, c, light, total, t=t):
+                total = [list(q) for q in total]
+                total[c][i] = total[c][i] + light * jnp.broadcast_to(a_ref[c, pl.ds(y * tiles + t, 1), :], (8, LANES))
+                return tuple(tuple(q) for q in total)
+
+            zero = jnp.zeros((8, LANES), jnp.float32)
+            view, total = march(table_ref, held_ref.at[t], local_ref.at[t], start, ny, add, ((zero, zero),) * 3)
+            lanes = slice(t * LANES, (t + 1) * LANES)
+            for i in range(2):
+                for c in range(3):
+                    out_ref[c, 8 * i : 8 * i + 8, lanes] = total[c][i]
+                out_ref[3, 8 * i : 8 * i + 8, lanes] = view[i]
+
+
+def pixels_of(own, before, table, held, local, view, ready, name):
+    tiles, nx, _, _ = held.shape
+    ny, nz = before.size // (2 * tiles * LANES), tiles * LANES
+    flat = (tiles, nx * PITCH, LANES)
     return pl.pallas_call(
         functools.partial(pixel_kernel, own, (nx, ny)),
-        in_specs=[VMEM] * 4,
+        in_specs=[VMEM] * 6,
         out_specs=VMEM,
         out_shape=jax.ShapeDtypeStruct((4, nx // 2, nz), jnp.float32),
         scratch_shapes=[pltpu.VMEM((3, ny * tiles, LANES), jnp.float32)],
         compiler_params=params(4),
         cost_estimate=cost(2**24, 2**22, 2**21),
         name=name,
-    )(table, before, held.reshape(flat), local.reshape(flat))
+    )(table, before, held.reshape(flat), local.reshape(flat), view, ready)
 
 
 def image_kernel(table_ref, kept_ref, received_ref, image_ref, passed_ref):
@@ -216,12 +265,12 @@
 def per_device(sizes, density, extinction, sun_colour, sky_colour):
     pairs, full_x, full_y = sizes
     deal = functools.partial(lax.all_to_all, split_axis=0, concat_axis=0, tiled=True)
-    column_light, table, held, local = load_of(density, extinction, sun_colour, sky_colour, full_x, full_y)
+    column_light, table, *brick = load_of(density, extinction, sun_colour, sky_colour, full_x, full_y)
     own = deal(column_light.reshape(pairs, -1, LANES), ("z", "y"))
     before = deal(before_of(own), ("z", "y", "x"))
-    sent = pixels_of(False, before, table, held, local, "pixels_sent")
+    sent = pixels_of(False, before, table, *brick, "pixels_sent")
     received = lax.ppermute(sent, "depth", [(0, 1), (1, 0)])
-    kept = pixels_of(True, before, table, held, local, "pixels_kept")
+    kept = pixels_of(True, before, table, *brick, "pixels_kept")
     return image_of(table, kept, received)
 
 

time: 52.3 us -> 49.5 us (0.946)
  blocking collectives: 39.7 us -> 35.8 us
  Pallas kernels: 7.94 us -> 8.78 us
    pallas_call x1, Pallas kernels: 2.68 us -> 6.8 us  [load_of(): pl.pallas_call(functools.partial(load_kernel, (nx, ny, full_x, full_y)),...]
    all_to_all x1, blocking collectives: 21.2 us -> 17.3 us  [per_device(): own = deal(column_light.reshape(pairs, -1, LANES), ('z', 'y'))]
    pallas_call x2, Pallas kernels: 4.49 us -> 1.23 us  [pixels_of(): pl.pallas_call(functools.partial(pixel_kernel, own, (nx, ny)), in_specs=[...]
  transfers between devices with their start and end apart: 1 -> 1, of which waited for: 0 -> 1; matrix products, arithmetic and copies ran while one was open for 0% -> 0% of each run, Pallas kernels for 4% -> 1%
where the time goes in v6:
time: 49.5 us; the launch traced here: 49.4 us
  blocking collectives  35.8 us (72%)
  Pallas kernels  8.78 us (18%)
  starting transfers between devices  3.82 us (8%)
  between operations  0.66 us (1%)
    all_to_all x1, blocking collectives, per_device(): before = deal(before_of(own), ('z', 'y', 'x'))  18.5 us
    all_to_all x1, blocking collectives, per_device(): own = deal(column_light.reshape(pairs, -1, LANES), ('z', 'y'))  17.3 us
    pallas_call x1, Pallas kernels, load_of(): pl.pallas_call(functools.partial(load_kernel, (nx, ny, full_x, full_y)),...  6.8 us
    ppermute x1, starting transfers between devices, per_device(): received = lax.ppermute(sent, 'depth', [(0, 1), (1, 0)])  3.82 us
    pallas_call x2, Pallas kernels, pixels_of(): pl.pallas_call(functools.partial(pixel_kernel, own, (nx, ny)), in_specs=[...  1.23 us
  transfers between devices with their start and end apart: 1, of which 1 were waited for; matrix products, arithmetic and copies ran while one was open for 0% of the time, Pallas kernels for 1%

profile of v6, /device:TPU:1, one launch (start us, length us, event | category | flops | bytes accessed | tf_op | source)
XLA Modules:
  0.0 49.4 jit_solution(9632681923886399700)
XLA Ops:
  0.6 6.8 %load.1 = (f32[256,128]{1,0:T(8,128)S(1)}, f32[96,128]{1,0:T(8,128)S(1)}, f32[4,32,72,128]{3,2,1,0:T(8,128)S(1)}, f32[4,32,72,128]{3,2,1,0:T(8,128)S(1)}, f32[32...) custom-call(f32[32,64,512]{2,1,0:T(8,128)} %density_ref.1, f32[3]{0:T(128)} %ext_ref.1, f32[3]{0:T(128)} %sun_ref.1, f32[3]{0:T(128)} %sky_ref.1), custom_call_target="tpu_custom_call" | custom-call | flops 2097152 | bytes 8388608 | tf_op jit(solution)/shard_map/load/pallas_call | solution.py:127
  7.4 17.3 %all_to_all.10.own_ref = f32[32,8,128]{2,1,0:T(8,128)S(1)} all-to-all(f32[32,8,128]{2,1,0:T(8,128)S(1)} %bitcast.7), channel_id=1, replica_groups=mesh['z'=8,'y'=4,'x'=2,'depth'=2,'tile'=2] {'z','y'}, dimensions={0} | all-to-all | bytes 262144 | tf_op jit(solution)/shard_map/all_to_all | solution.py:269
  24.7 18.5 %all_to_all.11.before_ref = f32[64,8,128]{2,1,0:T(8,128)S(1)} all-to-all(f32[64,8,128]{2,1,0:T(8,128)S(1)} %before.1), channel_id=1, replica_groups=mesh['z'=8,'y'=4,'x'=2,'depth'=2,'tile'=2] {'z','y','x'}, dimensions={0} | all-to-all | bytes 524288 | tf_op jit(solution)/shard_map/all_to_all | solution.py:270
  43.2 0.6 %pixels_sent.1 = f32[4,16,512]{2,1,0:T(8,128)S(1)} custom-call(f32[96,128]{1,0:T(8,128)S(1)} %get-tuple-element.8.table_ref, f32[64,8,128]{2,1,0:T(8,128)S(1)} %all_to_all.11.before_ref, f32[4,2304,128]{2,1,0:T(8,128)S(1)} %bitcast.3, f32[4,2304,128]{2,1,0:T(8,128)S(1)} %bitcast.5, f32[32,512]{1,0:T(8,128)S(1)} %get-tuple-element.12.view_ref, ...), custom_call_target="tpu_custom_call" | custom-call | flops 16777216 | bytes 4194304 | tf_op jit(solution)/shard_map/pixels_sent/pallas_call | solution.py:221
  43.9 3.8 %collective-permute-start = (f32[4,16,512]{2,1,0:T(8,128)S(1)}, f32[4,16,512]{2,1,0:T(8,128)S(1)}, u32[]{:S(2)}, u32[]{:S(2)}) collective-permute-start(f32[4,16,512]{2,1,0:T(8,128)S(1)} %pixels_sent.1), channel_id=1, source_target_pairs={{0,2},{2,0},{1,3},{3,1},{4,6},{6,4},{5,7},{7,5},{8,10},{10,8},{9,1... | collective-permute-start | bytes 393224 | tf_op jit(solution)/shard_map/ppermute | solution.py:272
  47.7 0.6 %pixels_kept.1.kept_ref = f32[4,16,512]{2,1,0:T(8,128)S(1)} custom-call(f32[96,128]{1,0:T(8,128)S(1)} %get-tuple-element.8.table_ref, f32[64,8,128]{2,1,0:T(8,128)S(1)} %all_to_all.11.before_ref, f32[4,2304,128]{2,1,0:T(8,128)S(1)} %bitcast.4, f32[4,2304,128]{2,1,0:T(8,128)S(1)} %bitcast.6, f32[32,512]{1,0:T(8,128)S(1)} %get-tuple-element.12.view_ref, ...), custom_call_target="tpu_custom_call" | custom-call | flops 16777216 | bytes 4194304 | tf_op jit(solution)/shard_map/pixels_kept/pallas_call | solution.py:221
  48.3 0.4 collective-permute-done.received_ref
  48.7 0.7 %image.1 = (f32[3,16,512]{2,1,0:T(8,128)}, f32[3,16,512]{2,1,0:T(8,128)}) custom-call(f32[96,128]{1,0:T(8,128)S(1)} %get-tuple-element.8.table_ref, f32[4,16,512]{2,1,0:T(8,128)S(1)} %pixels_kept.1.kept_ref, f32[4,16,512]{2,1,0:T(8,128)S(1)} %collective-permute-done.received_ref), custom_call_target="tpu_custom_call" | custom-call | tf_op jit(solution)/shard_map/image/pallas_call | solution.py:255
  (1 shorter events, 0.0 us)
Async XLA Ops:
  43.9 4.8 %collective-permute-start = (f32[4,16,512]{2,1,0:T(8,128)S(1)}, f32[4,16,512]{2,1,0:T(8,128)S(1)}, u32[]{:S(2)}, u32[]{:S(2)}) collective-permute-start(f32[4,16,512]{2,1,0:T(8,128)S(1)} %pixels_sent.1), channel_id=1, source_target_pairs={{0,2},{2,0},{1,3},{3,1},{4,6},{6,4},{5,7},{7,5},{8,10},{10,8},{9,1... | collective-permute-start | bytes 393224 | tf_op jit(solution)/shard_map/ppermute | solution.py:272

commit v7 on v6

--- a/solution.py
+++ b/solution.py
@@ -9,10 +9,9 @@
 from jax.sharding import PartitionSpec as P
 
 LANES = 128
-CHUNKS = 8
+CHUNKS = 4
 STEP = 8
 PITCH = 72
-AHEAD = 3
 WIDE = 32
 LOG2E = 1.4426950408889634
 VMEM = pl.BlockSpec(memory_space=pltpu.VMEM)
@@ -31,7 +30,13 @@
     return [pltpu.with_memory_space_constraint(x, pltpu.HBM) for x in arrays]
 
 
-def load_kernel(sizes, density_ref, ext_ref, sun_ref, sky_ref, light_ref, table_ref, held_ref, local_ref, view_ref, ready_ref, sums_ref, three_ref, sems, small_sems):
+def works_ahead():
+    z, y, x, tile = (lax.axis_index(axis) for axis in ("z", "y", "x", "tile"))
+    late = jnp.where(z < 4, 13 * z, 75 - 4 * z) + 9 * jnp.minimum(y, 2) + jnp.where(x == 0, 5 * tile, 21)
+    return late <= 55
+
+
+def load_kernel(sizes, density_ref, ext_ref, sun_ref, sky_ref, light_ref, table_ref, held_ref, local_ref, view_ref, ready_ref, sums_ref, columns_ref, three_ref, sems, small_sems):
     nx, ny, full_x, full_y = sizes
     tiles = held_ref.shape[0]
     planes = nx // CHUNKS
@@ -66,7 +71,9 @@
                     total = total + cell
                 sums_ref[t, at] = total
     for t in range(tiles):
-        light_ref[pl.ds(t, ny, stride=tiles), :] = sums_ref[t]
+        columns_ref[pl.ds(t, ny, stride=tiles), :] = sums_ref[t]
+    for k in range(light_ref.shape[0]):
+        light_ref[k] = columns_ref[8 * (k // 2) : 8 * (k // 2) + 8]
     for copy in small:
         copy.wait()
     for c in range(3):
@@ -74,7 +81,7 @@
         for i, value in enumerate(row):
             table_ref[8 * (4 * c + i) : 8 * (4 * c + i) + 8] = jnp.full((8, LANES), value, jnp.float32)
 
-    @pl.when(lax.axis_index("z") < AHEAD)
+    @pl.when(works_ahead())
     def _():
         flat = (nx * PITCH, LANES)
         for t in range(tiles):
@@ -129,7 +136,7 @@
         in_specs=[HBM, HBM, HBM, HBM],
         out_specs=[VMEM] * 6,
         out_shape=[
-            jax.ShapeDtypeStruct((ny * tiles, LANES), jnp.float32),
+            jax.ShapeDtypeStruct((ny * tiles // 4, 8, LANES), jnp.float32),
             jax.ShapeDtypeStruct((12 * 8, LANES), jnp.float32),
             held,
             held,
@@ -138,6 +145,7 @@
         ],
         scratch_shapes=[
             pltpu.VMEM((tiles, ny, LANES), jnp.float32),
+            pltpu.VMEM((ny * tiles, LANES), jnp.float32),
             pltpu.SMEM((3, 3), jnp.float32),
             pltpu.SemaphoreType.DMA((CHUNKS, tiles)),
             pltpu.SemaphoreType.DMA((3,)),
@@ -149,22 +157,21 @@
 
 
 def before_kernel(own_ref, dealt_ref):
-    near = (lax.axis_index("x") == 0).astype(jnp.float32)
+    far = (lax.axis_index("x") == 1).astype(jnp.float32)
     total = jnp.zeros_like(own_ref[0])
-    for k in range(own_ref.shape[0]):
-        own = own_ref[k]
-        dealt_ref[2 * k] = total
-        dealt_ref[2 * k + 1] = total + near * own
-        total = total + own
+    for k in range(dealt_ref.shape[0]):
+        near = own_ref[2 * k]
+        dealt_ref[k] = total + far * near
+        total = total + (near + own_ref[2 * k + 1])
 
 
 def before_of(own):
-    pairs, rows, lanes = own.shape
+    count, rows, lanes = own.shape
     return pl.pallas_call(
         before_kernel,
         in_specs=[VMEM],
         out_specs=VMEM,
-        out_shape=jax.ShapeDtypeStruct((2 * pairs, rows, lanes), jnp.float32),
+        out_shape=jax.ShapeDtypeStruct((count // 2, rows, lanes), jnp.float32),
         compiler_params=params(2),
         name="before",
     )(own)
@@ -176,11 +183,11 @@
     rows = nx // 2
     for c in range(3):
         rate, colour = factor(table_ref, c, 1), factor(table_ref, c, 2)
-        for k in range(before_ref.shape[0] // 2):
-            a_ref[c, 8 * k : 8 * k + 8] = colour * jnp.exp2((before_ref[2 * k] + before_ref[2 * k + 1]) * rate)
+        for k in range(before_ref.shape[0]):
+            a_ref[c, 8 * k : 8 * k + 8] = colour * jnp.exp2(before_ref[k] * rate)
     half = lax.axis_index("depth")
     start = (half if own else 1 - half) * rows
-    ahead = lax.axis_index("z") < AHEAD
+    ahead = works_ahead()
 
     @pl.when(ahead)
     def _():
@@ -216,7 +223,7 @@
 
 def pixels_of(own, before, table, held, local, view, ready, name):
     tiles, nx, _, _ = held.shape
-    ny, nz = before.size // (2 * tiles * LANES), tiles * LANES
+    ny, nz = before.size // (tiles * LANES), tiles * LANES
     flat = (tiles, nx * PITCH, LANES)
     return pl.pallas_call(
         functools.partial(pixel_kernel, own, (nx, ny)),
@@ -263,11 +270,10 @@
 
 
 def per_device(sizes, density, extinction, sun_colour, sky_colour):
-    pairs, full_x, full_y = sizes
+    full_x, full_y = sizes
     deal = functools.partial(lax.all_to_all, split_axis=0, concat_axis=0, tiled=True)
     column_light, table, *brick = load_of(density, extinction, sun_colour, sky_colour, full_x, full_y)
-    own = deal(column_light.reshape(pairs, -1, LANES), ("z", "y"))
-    before = deal(before_of(own), ("z", "y", "x"))
+    before = deal(before_of(deal(column_light, ("z", "y", "x"))), ("z", "y"))
     sent = pixels_of(False, before, table, *brick, "pixels_sent")
     received = lax.ppermute(sent, "depth", [(0, 1), (1, 0)])
     kept = pixels_of(True, before, table, *brick, "pixels_kept")
@@ -278,7 +284,7 @@
     shape = (8, 4, 2, 2, 2)
     light = ("z", "y", "x")
     fine = Mesh(mesh.devices.reshape(shape), (*light, "depth", "tile"))
-    sizes = (32, 2048, 128)
+    sizes = (2048, 128)
     return jax.shard_map(
         functools.partial(per_device, sizes),
         mesh=fine,

time: 49.5 us -> 50.7 us (1.024)
  blocking collectives: 35.8 us -> 38 us
  starting transfers between devices: 3.82 us -> 2.97 us
    all_to_all x2, blocking collectives: 35.8 us -> 38 us  [per_device(): before = deal(before_of(deal(column_light, ('z', 'y', 'x'))), ('z', 'y'))]
    ppermute x1, starting transfers between devices: 3.82 us -> 2.97 us  [per_device(): received = lax.ppermute(sent, 'depth', [(0, 1), (1, 0)])]
where the time goes in v7:
time: 50.7 us; the launch traced here: 50.6 us
  blocking collectives  38 us (75%)
  Pallas kernels  8.57 us (17%)
  starting transfers between devices  2.97 us (6%)
  between operations  0.66 us (1%)
    all_to_all x2, blocking collectives, per_device(): before = deal(before_of(deal(column_light, ('z', 'y', 'x'))), ('z', 'y'))  38 us
    pallas_call x1, Pallas kernels, load_of(): pl.pallas_call(functools.partial(load_kernel, (nx, ny, full_x, full_y)),...  6.59 us
    ppermute x1, starting transfers between devices, per_device(): received = lax.ppermute(sent, 'depth', [(0, 1), (1, 0)])  2.97 us
    pallas_call x2, Pallas kernels, pixels_of(): pl.pallas_call(functools.partial(pixel_kernel, own, (nx, ny)), in_specs=[...  1.23 us
  transfers between devices with their start and end apart: 1, of which 1 were waited for; matrix products, arithmetic and copies ran while one was open for 0% of the time, Pallas kernels for 1%

profile of v7, /device:TPU:1, one launch (start us, length us, event | category | flops | bytes accessed | tf_op | source)
XLA Modules:
  0.0 50.6 jit_solution(4364284413982370935)
XLA Ops:
  0.6 6.6 %load.1 = (f32[64,8,128]{2,1,0:T(8,128)S(1)}, f32[96,128]{1,0:T(8,128)S(1)}, f32[4,32,72,128]{3,2,1,0:T(8,128)S(1)}, f32[4,32,72,128]{3,2,1,0:T(8,128)S(1)}, f32...) custom-call(f32[32,64,512]{2,1,0:T(8,128)} %density_ref.1, f32[3]{0:T(128)} %ext_ref.1, f32[3]{0:T(128)} %sun_ref.1, ...), custom_call_target="tpu_custom_call" | custom-call | flops 2097152 | bytes 8388608 | tf_op jit(solution)/shard_map/load/pallas_call | solution.py:134
  7.2 22.9 %all_to_all.10.own_ref = f32[64,8,128]{2,1,0:T(8,128)S(1)} all-to-all(f32[64,8,128]{2,1,0:T(8,128)S(1)} %get-tuple-element.9), channel_id=1, replica_groups=mesh['z'=8,'y'=4,'x'=2,'depth'=2,'tile'=2] {'z','y','x'}, dimensions={0} | all-to-all | bytes 524288 | tf_op jit(solution)/shard_map/all_to_all | solution.py:276
  30.2 15.1 %all_to_all.11.before_ref = f32[32,8,128]{2,1,0:T(8,128)S(1)} all-to-all(f32[32,8,128]{2,1,0:T(8,128)S(1)} %before.1), channel_id=1, replica_groups=mesh['z'=8,'y'=4,'x'=2,'depth'=2,'tile'=2] {'z','y'}, dimensions={0} | all-to-all | bytes 262144 | tf_op jit(solution)/shard_map/all_to_all | solution.py:276
  45.3 0.6 %pixels_sent.1 = f32[4,16,512]{2,1,0:T(8,128)S(1)} custom-call(f32[96,128]{1,0:T(8,128)S(1)} %get-tuple-element.8.table_ref, f32[32,8,128]{2,1,0:T(8,128)S(1)} %all_to_all.11.before_ref, f32[4,2304,128]{2,1,0:T(8,128)S(1)} %bitcast.2, f32[4,2304,128]{2,1,0:T(8,128)S(1)} %bitcast.4, f32[32,512]{1,0:T(8,128)S(1)} %get-tuple-element.12.view_ref, ...), custom_call_target="tpu_custom_call" | custom-call | flops 16777216 | bytes 4194304 | tf_op jit(solution)/shard_map/pixels_sent/pallas_call | solution.py:228
  45.9 3.0 %collective-permute-start = (f32[4,16,512]{2,1,0:T(8,128)S(1)}, f32[4,16,512]{2,1,0:T(8,128)S(1)}, u32[]{:S(2)}, u32[]{:S(2)}) collective-permute-start(f32[4,16,512]{2,1,0:T(8,128)S(1)} %pixels_sent.1), channel_id=1, source_target_pairs={{0,2},{2,0},{1,3},{3,1},{4,6},{6,4},{5,7},{7,5},{8,10},{10,8},{9,1... | collective-permute-start | bytes 393224 | tf_op jit(solution)/shard_map/ppermute | solution.py:278
  48.9 0.6 %pixels_kept.1.kept_ref = f32[4,16,512]{2,1,0:T(8,128)S(1)} custom-call(f32[96,128]{1,0:T(8,128)S(1)} %get-tuple-element.8.table_ref, f32[32,8,128]{2,1,0:T(8,128)S(1)} %all_to_all.11.before_ref, f32[4,2304,128]{2,1,0:T(8,128)S(1)} %bitcast.3, f32[4,2304,128]{2,1,0:T(8,128)S(1)} %bitcast.5, f32[32,512]{1,0:T(8,128)S(1)} %get-tuple-element.12.view_ref, ...), custom_call_target="tpu_custom_call" | custom-call | flops 16777216 | bytes 4194304 | tf_op jit(solution)/shard_map/pixels_kept/pallas_call | solution.py:228
  49.5 0.4 collective-permute-done.received_ref
  49.8 0.7 %image.1 = (f32[3,16,512]{2,1,0:T(8,128)}, f32[3,16,512]{2,1,0:T(8,128)}) custom-call(f32[96,128]{1,0:T(8,128)S(1)} %get-tuple-element.8.table_ref, f32[4,16,512]{2,1,0:T(8,128)S(1)} %pixels_kept.1.kept_ref, f32[4,16,512]{2,1,0:T(8,128)S(1)} %collective-permute-done.received_ref), custom_call_target="tpu_custom_call" | custom-call | tf_op jit(solution)/shard_map/image/pallas_call | solution.py:262
  (1 shorter events, 0.0 us)
Async XLA Ops:
  45.9 4.0 %collective-permute-start = (f32[4,16,512]{2,1,0:T(8,128)S(1)}, f32[4,16,512]{2,1,0:T(8,128)S(1)}, u32[]{:S(2)}, u32[]{:S(2)}) collective-permute-start(f32[4,16,512]{2,1,0:T(8,128)S(1)} %pixels_sent.1), channel_id=1, source_target_pairs={{0,2},{2,0},{1,3},{3,1},{4,6},{6,4},{5,7},{7,5},{8,10},{10,8},{9,1... | collective-permute-start | bytes 393224 | tf_op jit(solution)/shard_map/ppermute | solution.py:278

commit v8 on v6

--- a/solution.py
+++ b/solution.py
@@ -9,10 +9,9 @@
 from jax.sharding import PartitionSpec as P
 
 LANES = 128
-CHUNKS = 8
+CHUNKS = 4
 STEP = 8
 PITCH = 72
-AHEAD = 3
 WIDE = 32
 LOG2E = 1.4426950408889634
 VMEM = pl.BlockSpec(memory_space=pltpu.VMEM)
@@ -29,6 +28,12 @@
 
 def in_hbm(*arrays):
     return [pltpu.with_memory_space_constraint(x, pltpu.HBM) for x in arrays]
+
+
+def works_ahead():
+    z, y, x, tile = (lax.axis_index(axis) for axis in ("z", "y", "x", "tile"))
+    late = jnp.where(z < 4, 13 * z, 75 - 4 * z) + 9 * jnp.minimum(y, 2) + jnp.where(x == 0, 5 * tile, 21)
+    return late <= 55
 
 
 def load_kernel(sizes, density_ref, ext_ref, sun_ref, sky_ref, light_ref, table_ref, held_ref, local_ref, view_ref, ready_ref, sums_ref, three_ref, sems, small_sems):
@@ -74,7 +79,7 @@
         for i, value in enumerate(row):
             table_ref[8 * (4 * c + i) : 8 * (4 * c + i) + 8] = jnp.full((8, LANES), value, jnp.float32)
 
-    @pl.when(lax.axis_index("z") < AHEAD)
+    @pl.when(works_ahead())
     def _():
         flat = (nx * PITCH, LANES)
         for t in range(tiles):
@@ -180,7 +185,7 @@
             a_ref[c, 8 * k : 8 * k + 8] = colour * jnp.exp2((before_ref[2 * k] + before_ref[2 * k + 1]) * rate)
     half = lax.axis_index("depth")
     start = (half if own else 1 - half) * rows
-    ahead = lax.axis_index("z") < AHEAD
+    ahead = works_ahead()
 
     @pl.when(ahead)
     def _():
@@ -263,10 +268,10 @@
 
 
 def per_device(sizes, density, extinction, sun_colour, sky_colour):
-    pairs, full_x, full_y = sizes
+    full_x, full_y = sizes
     deal = functools.partial(lax.all_to_all, split_axis=0, concat_axis=0, tiled=True)
     column_light, table, *brick = load_of(density, extinction, sun_colour, sky_colour, full_x, full_y)
-    own = deal(column_light.reshape(pairs, -1, LANES), ("z", "y"))
+    own = deal(column_light.reshape(-1, 8, LANES), ("z", "y"))
     before = deal(before_of(own), ("z", "y", "x"))
     sent = pixels_of(False, before, table, *brick, "pixels_sent")
     received = lax.ppermute(sent, "depth", [(0, 1), (1, 0)])
@@ -278,7 +283,7 @@
     shape = (8, 4, 2, 2, 2)
     light = ("z", "y", "x")
     fine = Mesh(mesh.devices.reshape(shape), (*light, "depth", "tile"))
-    sizes = (32, 2048, 128)
+    sizes = (2048, 128)
     return jax.shard_map(
         functools.partial(per_device, sizes),
         mesh=fine,

time: 49.5 us -> 49.1 us (level)
    all_to_all x1, blocking collectives: 18.5 us -> 17.5 us  [per_device(): before = deal(before_of(own), ('z', 'y', 'x'))]
    all_to_all x1, blocking collectives: 17.3 us -> 18.1 us  [per_device(): own = deal(column_light.reshape(-1, 8, LANES), ('z', 'y'))]
where the time goes in v8:
time: 49.1 us; the launch traced here: 49 us
  blocking collectives  35.6 us (73%)
  Pallas kernels  8.56 us (17%)
  starting transfers between devices  3.82 us (8%)
  between operations  0.66 us (1%)
    all_to_all x1, blocking collectives, per_device(): own = deal(column_light.reshape(-1, 8, LANES), ('z', 'y'))  18.1 us
    all_to_all x1, blocking collectives, per_device(): before = deal(before_of(own), ('z', 'y', 'x'))  17.5 us
    pallas_call x1, Pallas kernels, load_of(): pl.pallas_call(functools.partial(load_kernel, (nx, ny, full_x, full_y)),...  6.57 us
    ppermute x1, starting transfers between devices, per_device(): received = lax.ppermute(sent, 'depth', [(0, 1), (1, 0)])  3.82 us
    pallas_call x2, Pallas kernels, pixels_of(): pl.pallas_call(functools.partial(pixel_kernel, own, (nx, ny)), in_specs=[...  1.23 us
  transfers between devices with their start and end apart: 1, of which 1 were waited for; matrix products, arithmetic and copies ran while one was open for 0% of the time, Pallas kernels for 1%

profile of v8, /device:TPU:1, one launch (start us, length us, event | category | flops | bytes accessed | tf_op | source)
XLA Modules:
  0.0 49.0 jit_solution(16288540727172170065)
XLA Ops:
  0.6 6.6 %load.1 = (f32[256,128]{1,0:T(8,128)S(1)}, f32[96,128]{1,0:T(8,128)S(1)}, f32[4,32,72,128]{3,2,1,0:T(8,128)S(1)}, f32[4,32,72,128]{3,2,1,0:T(8,128)S(1)}, f32[32...) custom-call(f32[32,64,512]{2,1,0:T(8,128)} %density_ref.1, f32[3]{0:T(128)} %ext_ref.1, f32[3]{0:T(128)} %sun_ref.1, f32[3]{0:T(128)} %sky_ref.1), custom_call_target="tpu_custom_call" | custom-call | flops 2097152 | bytes 8388608 | tf_op jit(solution)/shard_map/load/pallas_call | solution.py:132
  7.2 18.1 %all_to_all.10.own_ref = f32[32,8,128]{2,1,0:T(8,128)S(1)} all-to-all(f32[32,8,128]{2,1,0:T(8,128)S(1)} %bitcast.7), channel_id=1, replica_groups=mesh['z'=8,'y'=4,'x'=2,'depth'=2,'tile'=2] {'z','y'}, dimensions={0} | all-to-all | bytes 262144 | tf_op jit(solution)/shard_map/all_to_all | solution.py:274
  25.4 17.5 %all_to_all.11.before_ref = f32[64,8,128]{2,1,0:T(8,128)S(1)} all-to-all(f32[64,8,128]{2,1,0:T(8,128)S(1)} %before.1), channel_id=1, replica_groups=mesh['z'=8,'y'=4,'x'=2,'depth'=2,'tile'=2] {'z','y','x'}, dimensions={0} | all-to-all | bytes 524288 | tf_op jit(solution)/shard_map/all_to_all | solution.py:275
  42.8 0.6 %pixels_sent.1 = f32[4,16,512]{2,1,0:T(8,128)S(1)} custom-call(f32[96,128]{1,0:T(8,128)S(1)} %get-tuple-element.8.table_ref, f32[64,8,128]{2,1,0:T(8,128)S(1)} %all_to_all.11.before_ref, f32[4,2304,128]{2,1,0:T(8,128)S(1)} %bitcast.3, f32[4,2304,128]{2,1,0:T(8,128)S(1)} %bitcast.5, f32[32,512]{1,0:T(8,128)S(1)} %get-tuple-element.12.view_ref, ...), custom_call_target="tpu_custom_call" | custom-call | flops 16777216 | bytes 4194304 | tf_op jit(solution)/shard_map/pixels_sent/pallas_call | solution.py:226
  43.4 3.8 %collective-permute-start = (f32[4,16,512]{2,1,0:T(8,128)S(1)}, f32[4,16,512]{2,1,0:T(8,128)S(1)}, u32[]{:S(2)}, u32[]{:S(2)}) collective-permute-start(f32[4,16,512]{2,1,0:T(8,128)S(1)} %pixels_sent.1), channel_id=1, source_target_pairs={{0,2},{2,0},{1,3},{3,1},{4,6},{6,4},{5,7},{7,5},{8,10},{10,8},{9,1... | collective-permute-start | bytes 393224 | tf_op jit(solution)/shard_map/ppermute | solution.py:277
  47.3 0.6 %pixels_kept.1.kept_ref = f32[4,16,512]{2,1,0:T(8,128)S(1)} custom-call(f32[96,128]{1,0:T(8,128)S(1)} %get-tuple-element.8.table_ref, f32[64,8,128]{2,1,0:T(8,128)S(1)} %all_to_all.11.before_ref, f32[4,2304,128]{2,1,0:T(8,128)S(1)} %bitcast.4, f32[4,2304,128]{2,1,0:T(8,128)S(1)} %bitcast.6, f32[32,512]{1,0:T(8,128)S(1)} %get-tuple-element.12.view_ref, ...), custom_call_target="tpu_custom_call" | custom-call | flops 16777216 | bytes 4194304 | tf_op jit(solution)/shard_map/pixels_kept/pallas_call | solution.py:226
  47.9 0.4 collective-permute-done.received_ref
  48.3 0.7 %image.1 = (f32[3,16,512]{2,1,0:T(8,128)}, f32[3,16,512]{2,1,0:T(8,128)}) custom-call(f32[96,128]{1,0:T(8,128)S(1)} %get-tuple-element.8.table_ref, f32[4,16,512]{2,1,0:T(8,128)S(1)} %pixels_kept.1.kept_ref, f32[4,16,512]{2,1,0:T(8,128)S(1)} %collective-permute-done.received_ref), custom_call_target="tpu_custom_call" | custom-call | tf_op jit(solution)/shard_map/image/pallas_call | solution.py:260
  (1 shorter events, 0.0 us)
Async XLA Ops:
  43.4 4.8 %collective-permute-start = (f32[4,16,512]{2,1,0:T(8,128)S(1)}, f32[4,16,512]{2,1,0:T(8,128)S(1)}, u32[]{:S(2)}, u32[]{:S(2)}) collective-permute-start(f32[4,16,512]{2,1,0:T(8,128)S(1)} %pixels_sent.1), channel_id=1, source_target_pairs={{0,2},{2,0},{1,3},{3,1},{4,6},{6,4},{5,7},{7,5},{8,10},{10,8},{9,1... | collective-permute-start | bytes 393224 | tf_op jit(solution)/shard_map/ppermute | solution.py:277

commit v9 on v8

--- a/solution.py
+++ b/solution.py
@@ -12,6 +12,7 @@
 CHUNKS = 4
 STEP = 8
 PITCH = 72
+COLUMNS = 4
 WIDE = 32
 LOG2E = 1.4426950408889634
 VMEM = pl.BlockSpec(memory_space=pltpu.VMEM)
@@ -153,13 +154,19 @@
     )(*in_hbm(density, extinction, sun_colour, sky_colour))
 
 
+def place(k, pairs):
+    z, y = divmod(k, COLUMNS)
+    return 2 * (y * (pairs // COLUMNS) + z)
+
+
 def before_kernel(own_ref, dealt_ref):
     near = (lax.axis_index("x") == 0).astype(jnp.float32)
     total = jnp.zeros_like(own_ref[0])
     for k in range(own_ref.shape[0]):
         own = own_ref[k]
-        dealt_ref[2 * k] = total
-        dealt_ref[2 * k + 1] = total + near * own
+        at = place(k, own_ref.shape[0])
+        dealt_ref[at] = total
+        dealt_ref[at + 1] = total + near * own
         total = total + own
 
 
@@ -182,7 +189,8 @@
     for c in range(3):
         rate, colour = factor(table_ref, c, 1), factor(table_ref, c, 2)
         for k in range(before_ref.shape[0] // 2):
-            a_ref[c, 8 * k : 8 * k + 8] = colour * jnp.exp2((before_ref[2 * k] + before_ref[2 * k + 1]) * rate)
+            at = place(k, before_ref.shape[0] // 2)
+            a_ref[c, 8 * k : 8 * k + 8] = colour * jnp.exp2((before_ref[at] + before_ref[at + 1]) * rate)
     half = lax.axis_index("depth")
     start = (half if own else 1 - half) * rows
     ahead = works_ahead()
@@ -272,7 +280,7 @@
     deal = functools.partial(lax.all_to_all, split_axis=0, concat_axis=0, tiled=True)
     column_light, table, *brick = load_of(density, extinction, sun_colour, sky_colour, full_x, full_y)
     own = deal(column_light.reshape(-1, 8, LANES), ("z", "y"))
-    before = deal(before_of(own), ("z", "y", "x"))
+    before = deal(before_of(own), ("y", "z", "x"))
     sent = pixels_of(False, before, table, *brick, "pixels_sent")
     received = lax.ppermute(sent, "depth", [(0, 1), (1, 0)])
     kept = pixels_of(True, before, table, *brick, "pixels_kept")

time: 49.1 us -> 48.6 us (0.990)
  blocking collectives: 35.6 us -> 34.9 us
    all_to_all x1, blocking collectives: 17.5 us -> 16.8 us  [per_device(): before = deal(before_of(own), ('y', 'z', 'x'))]
where the time goes in v9:
time: 48.6 us; the launch traced here: 48.5 us
  blocking collectives  34.9 us (72%)
  Pallas kernels  8.56 us (18%)
  starting transfers between devices  4 us (8%)
  between operations  0.66 us (1%)
    all_to_all x1, blocking collectives, per_device(): own = deal(column_light.reshape(-1, 8, LANES), ('z', 'y'))  18.1 us
    all_to_all x1, blocking collectives, per_device(): before = deal(before_of(own), ('y', 'z', 'x'))  16.8 us
    pallas_call x1, Pallas kernels, load_of(): pl.pallas_call(functools.partial(load_kernel, (nx, ny, full_x, full_y)),...  6.57 us
    ppermute x1, starting transfers between devices, per_device(): received = lax.ppermute(sent, 'depth', [(0, 1), (1, 0)])  4 us
    pallas_call x2, Pallas kernels, pixels_of(): pl.pallas_call(functools.partial(pixel_kernel, own, (nx, ny)), in_specs=[...  1.23 us
  transfers between devices with their start and end apart: 1, of which 1 were waited for; matrix products, arithmetic and copies ran while one was open for 0% of the time, Pallas kernels for 1%

profile of v9, /device:TPU:1, one launch (start us, length us, event | category | flops | bytes accessed | tf_op | source)
XLA Modules:
  0.0 48.5 jit_solution(8537467391121616626)
XLA Ops:
  0.6 6.6 %load.1 = (f32[256,128]{1,0:T(8,128)S(1)}, f32[96,128]{1,0:T(8,128)S(1)}, f32[4,32,72,128]{3,2,1,0:T(8,128)S(1)}, f32[4,32,72,128]{3,2,1,0:T(8,128)S(1)}, f32[32...) custom-call(f32[32,64,512]{2,1,0:T(8,128)} %density_ref.1, f32[3]{0:T(128)} %ext_ref.1, f32[3]{0:T(128)} %sun_ref.1, f32[3]{0:T(128)} %sky_ref.1), custom_call_target="tpu_custom_call" | custom-call | flops 2097152 | bytes 8388608 | tf_op jit(solution)/shard_map/load/pallas_call | solution.py:133
  7.2 18.1 %all_to_all.10.own_ref = f32[32,8,128]{2,1,0:T(8,128)S(1)} all-to-all(f32[32,8,128]{2,1,0:T(8,128)S(1)} %bitcast.7), channel_id=1, replica_groups=mesh['z'=8,'y'=4,'x'=2,'depth'=2,'tile'=2] {'z','y'}, dimensions={0} | all-to-all | bytes 262144 | tf_op jit(solution)/shard_map/all_to_all | solution.py:282
  25.4 16.8 %all_to_all.11.before_ref = f32[64,8,128]{2,1,0:T(8,128)S(1)} all-to-all(f32[64,8,128]{2,1,0:T(8,128)S(1)} %before.1), channel_id=1, replica_groups=mesh['z'=8,'y'=4,'x'=2,'depth'=2,'tile'=2] {'y','z','x'}, dimensions={0} | all-to-all | bytes 524288 | tf_op jit(solution)/shard_map/all_to_all | solution.py:283
  42.1 0.6 %pixels_sent.1 = f32[4,16,512]{2,1,0:T(8,128)S(1)} custom-call(f32[96,128]{1,0:T(8,128)S(1)} %get-tuple-element.8.table_ref, f32[64,8,128]{2,1,0:T(8,128)S(1)} %all_to_all.11.before_ref, f32[4,2304,128]{2,1,0:T(8,128)S(1)} %bitcast.3, f32[4,2304,128]{2,1,0:T(8,128)S(1)} %bitcast.5, f32[32,512]{1,0:T(8,128)S(1)} %get-tuple-element.12.view_ref, ...), custom_call_target="tpu_custom_call" | custom-call | flops 16777216 | bytes 4194304 | tf_op jit(solution)/shard_map/pixels_sent/pallas_call | solution.py:234
  42.8 4.0 %collective-permute-start = (f32[4,16,512]{2,1,0:T(8,128)S(1)}, f32[4,16,512]{2,1,0:T(8,128)S(1)}, u32[]{:S(2)}, u32[]{:S(2)}) collective-permute-start(f32[4,16,512]{2,1,0:T(8,128)S(1)} %pixels_sent.1), channel_id=1, source_target_pairs={{0,2},{2,0},{1,3},{3,1},{4,6},{6,4},{5,7},{7,5},{8,10},{10,8},{9,1... | collective-permute-start | bytes 393224 | tf_op jit(solution)/shard_map/ppermute | solution.py:285
  46.8 0.6 %pixels_kept.1.kept_ref = f32[4,16,512]{2,1,0:T(8,128)S(1)} custom-call(f32[96,128]{1,0:T(8,128)S(1)} %get-tuple-element.8.table_ref, f32[64,8,128]{2,1,0:T(8,128)S(1)} %all_to_all.11.before_ref, f32[4,2304,128]{2,1,0:T(8,128)S(1)} %bitcast.4, f32[4,2304,128]{2,1,0:T(8,128)S(1)} %bitcast.6, f32[32,512]{1,0:T(8,128)S(1)} %get-tuple-element.12.view_ref, ...), custom_call_target="tpu_custom_call" | custom-call | flops 16777216 | bytes 4194304 | tf_op jit(solution)/shard_map/pixels_kept/pallas_call | solution.py:234
  47.4 0.4 collective-permute-done.received_ref
  47.7 0.7 %image.1 = (f32[3,16,512]{2,1,0:T(8,128)}, f32[3,16,512]{2,1,0:T(8,128)}) custom-call(f32[96,128]{1,0:T(8,128)S(1)} %get-tuple-element.8.table_ref, f32[4,16,512]{2,1,0:T(8,128)S(1)} %pixels_kept.1.kept_ref, f32[4,16,512]{2,1,0:T(8,128)S(1)} %collective-permute-done.received_ref), custom_call_target="tpu_custom_call" | custom-call | tf_op jit(solution)/shard_map/image/pallas_call | solution.py:268
  (1 shorter events, 0.0 us)
Async XLA Ops:
  42.8 5.0 %collective-permute-start = (f32[4,16,512]{2,1,0:T(8,128)S(1)}, f32[4,16,512]{2,1,0:T(8,128)S(1)}, u32[]{:S(2)}, u32[]{:S(2)}) collective-permute-start(f32[4,16,512]{2,1,0:T(8,128)S(1)} %pixels_sent.1), channel_id=1, source_target_pairs={{0,2},{2,0},{1,3},{3,1},{4,6},{6,4},{5,7},{7,5},{8,10},{10,8},{9,1... | collective-permute-start | bytes 393224 | tf_op jit(solution)/shard_map/ppermute | solution.py:285

commit v10 on v8

--- a/solution.py
+++ b/solution.py
@@ -5,13 +5,13 @@
 from jax import lax
 from jax.experimental import pallas as pl
 from jax.experimental.pallas import tpu as pltpu
-from jax.sharding import Mesh
 from jax.sharding import PartitionSpec as P
 
 LANES = 128
 CHUNKS = 4
 STEP = 8
 PITCH = 72
+COLUMNS = 4
 WIDE = 32
 LOG2E = 1.4426950408889634
 VMEM = pl.BlockSpec(memory_space=pltpu.VMEM)
@@ -30,8 +30,14 @@
     return [pltpu.with_memory_space_constraint(x, pltpu.HBM) for x in arrays]
 
 
+def light_place():
+    light = lax.axis_index("light")
+    return light // (2 * COLUMNS), light // 2 % COLUMNS, light % 2
+
+
 def works_ahead():
-    z, y, x, tile = (lax.axis_index(axis) for axis in ("z", "y", "x", "tile"))
+    z, y, x = light_place()
+    tile = lax.axis_index("tile")
     late = jnp.where(z < 4, 13 * z, 75 - 4 * z) + 9 * jnp.minimum(y, 2) + jnp.where(x == 0, 5 * tile, 21)
     return late <= 55
 
@@ -153,13 +159,21 @@
     )(*in_hbm(density, extinction, sun_colour, sky_colour))
 
 
+def second_round():
+    return sorted(range(64), key=lambda i: (i // 2 % COLUMNS, i // 8, i % 2))[::-1]
+
+
+def place(k, x):
+    return second_round().index(2 * k + x)
+
+
 def before_kernel(own_ref, dealt_ref):
-    near = (lax.axis_index("x") == 0).astype(jnp.float32)
+    near = (light_place()[2] == 0).astype(jnp.float32)
     total = jnp.zeros_like(own_ref[0])
     for k in range(own_ref.shape[0]):
-        own = own_ref[k]
-        dealt_ref[2 * k] = total
-        dealt_ref[2 * k + 1] = total + near * own
+        own = own_ref[own_ref.shape[0] - 1 - k]
+        dealt_ref[place(k, 0)] = total
+        dealt_ref[place(k, 1)] = total + near * own
         total = total + own
 
 
@@ -182,7 +196,9 @@
     for c in range(3):
         rate, colour = factor(table_ref, c, 1), factor(table_ref, c, 2)
         for k in range(before_ref.shape[0] // 2):
-            a_ref[c, 8 * k : 8 * k + 8] = colour * jnp.exp2((before_ref[2 * k] + before_ref[2 * k + 1]) * rate)
+            column = before_ref[place(k, 0)] + before_ref[place(k, 1)]
+            row = 8 * (before_ref.shape[0] // 2 - 1 - k)
+            a_ref[c, row : row + 8] = colour * jnp.exp2(column * rate)
     half = lax.axis_index("depth")
     start = (half if own else 1 - half) * rows
     ahead = works_ahead()
@@ -269,10 +285,11 @@
 
 def per_device(sizes, density, extinction, sun_colour, sky_colour):
     full_x, full_y = sizes
-    deal = functools.partial(lax.all_to_all, split_axis=0, concat_axis=0, tiled=True)
+    deal = functools.partial(lax.all_to_all, axis_name="light", split_axis=0, concat_axis=0, tiled=True)
     column_light, table, *brick = load_of(density, extinction, sun_colour, sky_colour, full_x, full_y)
-    own = deal(column_light.reshape(-1, 8, LANES), ("z", "y"))
-    before = deal(before_of(own), ("z", "y", "x"))
+    count = lax.axis_size("light")
+    own = deal(column_light.reshape(-1, 8, LANES), axis_index_groups=[list(range(x, count, 2))[::-1] for x in range(2)])
+    before = deal(before_of(own), axis_index_groups=[second_round()])
     sent = pixels_of(False, before, table, *brick, "pixels_sent")
     received = lax.ppermute(sent, "depth", [(0, 1), (1, 0)])
     kept = pixels_of(True, before, table, *brick, "pixels_kept")
@@ -280,14 +297,11 @@
 
 
 def solution(mesh):
-    shape = (8, 4, 2, 2, 2)
-    light = ("z", "y", "x")
-    fine = Mesh(mesh.devices.reshape(shape), (*light, "depth", "tile"))
     sizes = (2048, 128)
     return jax.shard_map(
         functools.partial(per_device, sizes),
-        mesh=fine,
-        in_specs=(P(light, "depth", "tile"), P(), P(), P()),
-        out_specs=(P(None, (*light, "depth"), "tile"), P(None, (*light, "depth"), "tile")),
+        mesh=mesh,
+        in_specs=(P("light", "depth", "tile"), P(), P(), P()),
+        out_specs=(P(None, ("light", "depth"), "tile"), P(None, ("light", "depth"), "tile")),
         check_vma=False,
     )

time: 49.1 us -> 47.7 us (0.971)
  blocking collectives: 35.6 us -> 34.3 us
    all_to_all x2, blocking collectives: 35.6 us -> 34.3 us  [the longest x1 17.5 us: per_device(): deal(column_light.reshape(-1, 8, LANES), axis_index_groups=[list(range(x,...]
where the time goes in v10:
time: 47.7 us; the launch traced here: 47.3 us
  blocking collectives  34.3 us (72%)
  Pallas kernels  8.56 us (18%)
  starting transfers between devices  3.49 us (7%)
  between operations  0.66 us (1%)
    all_to_all x1, blocking collectives, per_device(): deal(column_light.reshape(-1, 8, LANES), axis_index_groups=[list(range(x,...  17.5 us
    all_to_all x1, blocking collectives, per_device(): before = deal(before_of(own), axis_index_groups=[second_round()])  16.7 us
    pallas_call x1, Pallas kernels, load_of(): pl.pallas_call(functools.partial(load_kernel, (nx, ny, full_x, full_y)),...  6.58 us
    ppermute x1, starting transfers between devices, per_device(): received = lax.ppermute(sent, 'depth', [(0, 1), (1, 0)])  3.49 us
    pallas_call x2, Pallas kernels, pixels_of(): pl.pallas_call(functools.partial(pixel_kernel, own, (nx, ny)), in_specs=[...  1.23 us
  transfers between devices with their start and end apart: 1, of which 1 were waited for; matrix products, arithmetic and copies ran while one was open for 0% of the time, Pallas kernels for 1%

profile of v10, /device:TPU:1, one launch (start us, length us, event | category | flops | bytes accessed | tf_op | source)
XLA Modules:
  0.0 47.3 jit_solution(13784457623888964256)
XLA Ops:
  0.6 6.6 %load.1 = (f32[256,128]{1,0:T(8,128)S(1)}, f32[96,128]{1,0:T(8,128)S(1)}, f32[4,32,72,128]{3,2,1,0:T(8,128)S(1)}, f32[4,32,72,128]{3,2,1,0:T(8,128)S(1)}, f32[32...) custom-call(f32[32,64,512]{2,1,0:T(8,128)} %density_ref.1, f32[3]{0:T(128)} %ext_ref.1, f32[3]{0:T(128)} %sun_ref.1, f32[3]{0:T(128)} %sky_ref.1), custom_call_target="tpu_custom_call" | custom-call | flops 2097152 | bytes 8388608 | tf_op jit(solution)/shard_map/load/pallas_call | solution.py:138
  7.2 17.5 %all_to_all.10.own_ref = f32[32,8,128]{2,1,0:T(8,128)S(1)} all-to-all(f32[32,8,128]{2,1,0:T(8,128)S(1)} %bitcast.7), channel_id=1, replica_groups={{248,240,232,224,216,208,200,192,184,176,168,160,152,144,136,128,120,11..., dimensions={0} | all-to-all | bytes 262144 | tf_op jit(solution)/shard_map/all_to_all | solution.py:291
  24.8 16.7 %all_to_all.11.before_ref = f32[64,8,128]{2,1,0:T(8,128)S(1)} all-to-all(f32[64,8,128]{2,1,0:T(8,128)S(1)} %before.1), channel_id=1, replica_groups={{252,248,220,216,188,184,156,152,124,120,92,88,60,56,28,24,244,240,212,..., dimensions={0} | all-to-all | bytes 524288 | tf_op jit(solution)/shard_map/all_to_all | solution.py:292
  41.5 0.6 %pixels_sent.1 = f32[4,16,512]{2,1,0:T(8,128)S(1)} custom-call(f32[96,128]{1,0:T(8,128)S(1)} %get-tuple-element.8.table_ref, f32[64,8,128]{2,1,0:T(8,128)S(1)} %all_to_all.11.before_ref, f32[4,2304,128]{2,1,0:T(8,128)S(1)} %bitcast.3, f32[4,2304,128]{2,1,0:T(8,128)S(1)} %bitcast.5, f32[32,512]{1,0:T(8,128)S(1)} %get-tuple-element.12.view_ref, ...), custom_call_target="tpu_custom_call" | custom-call | flops 16777216 | bytes 4194304 | tf_op jit(solution)/shard_map/pixels_sent/pallas_call | solution.py:242
  42.1 3.5 %collective-permute-start = (f32[4,16,512]{2,1,0:T(8,128)S(1)}, f32[4,16,512]{2,1,0:T(8,128)S(1)}, u32[]{:S(2)}, u32[]{:S(2)}) collective-permute-start(f32[4,16,512]{2,1,0:T(8,128)S(1)} %pixels_sent.1), channel_id=1, source_target_pairs={{0,2},{2,0},{1,3},{3,1},{4,6},{6,4},{5,7},{7,5},{8,10},{10,8},{9,1... | collective-permute-start | bytes 393224 | tf_op jit(solution)/shard_map/ppermute | solution.py:294
  45.6 0.6 %pixels_kept.1.kept_ref = f32[4,16,512]{2,1,0:T(8,128)S(1)} custom-call(f32[96,128]{1,0:T(8,128)S(1)} %get-tuple-element.8.table_ref, f32[64,8,128]{2,1,0:T(8,128)S(1)} %all_to_all.11.before_ref, f32[4,2304,128]{2,1,0:T(8,128)S(1)} %bitcast.4, f32[4,2304,128]{2,1,0:T(8,128)S(1)} %bitcast.6, f32[32,512]{1,0:T(8,128)S(1)} %get-tuple-element.12.view_ref, ...), custom_call_target="tpu_custom_call" | custom-call | flops 16777216 | bytes 4194304 | tf_op jit(solution)/shard_map/pixels_kept/pallas_call | solution.py:242
  46.3 0.4 collective-permute-done.received_ref
  46.6 0.7 %image.1 = (f32[3,16,512]{2,1,0:T(8,128)}, f32[3,16,512]{2,1,0:T(8,128)}) custom-call(f32[96,128]{1,0:T(8,128)S(1)} %get-tuple-element.8.table_ref, f32[4,16,512]{2,1,0:T(8,128)S(1)} %pixels_kept.1.kept_ref, f32[4,16,512]{2,1,0:T(8,128)S(1)} %collective-permute-done.received_ref), custom_call_target="tpu_custom_call" | custom-call | tf_op jit(solution)/shard_map/image/pallas_call | solution.py:276
  (1 shorter events, 0.0 us)
Async XLA Ops:
  42.1 4.5 %collective-permute-start = (f32[4,16,512]{2,1,0:T(8,128)S(1)}, f32[4,16,512]{2,1,0:T(8,128)S(1)}, u32[]{:S(2)}, u32[]{:S(2)}) collective-permute-start(f32[4,16,512]{2,1,0:T(8,128)S(1)} %pixels_sent.1), channel_id=1, source_target_pairs={{0,2},{2,0},{1,3},{3,1},{4,6},{6,4},{5,7},{7,5},{8,10},{10,8},{9,1... | collective-permute-start | bytes 393224 | tf_op jit(solution)/shard_map/ppermute | solution.py:294
